TPU v7x, 128 devices: a whole 4x4x4 slice. The times are simulated.
128 devices in a mesh: dp: 16 (over y, x_hi, core), tensor: 8 (over x_lo, z).
Axes of the slice: x: 4 (x_hi: 2, x_lo: 2; x = x_hi * 2 + x_lo), y: 4, z: 4, core: 2. Of those that a mesh axis runs over, the one named last changes fastest.
Arguments:
- tokens: bfloat16 [16384, 2048], P(('dp', 'tensor')), may hold values from -6 to 6
- lengths: int32 [16, 8], P('dp'), may hold values from 1 to 512, 1024 in all within a row
- attn_gain: float32 [2048], replicated, may hold values from 0.5 to 1.5
- query_weight: bfloat16 [2048, 2048], P('dp', 'tensor'), may hold values from -0.125 to 0.125
- key_weight: bfloat16 [2048, 2048], P('dp', 'tensor'), may hold values from -0.125 to 0.125
- value_weight: bfloat16 [2048, 2048], P('dp', 'tensor'), may hold values from -0.125 to 0.125
- out_weight: bfloat16 [2048, 2048], P('dp', 'tensor'), may hold values from -1 to 1
- mlp_gain: float32 [2048], replicated, may hold values from 0.5 to 1.5
- gate_weight: bfloat16 [2048, 5504], P('dp', 'tensor'), may hold values from -0.125 to 0.125
- up_weight: bfloat16 [2048, 5504], P('dp', 'tensor'), may hold values from -0.125 to 0.125
- down_weight: bfloat16 [2048, 5504], P('dp', 'tensor'), may hold values from -0.078125 to 0.078125
- cotangent: bfloat16 [16384, 2048], P(('dp', 'tensor')), may hold values from -6 to 6
Outputs:
- mixed: bfloat16 [16384, 2048], P(('dp', 'tensor'))
- tokens_grad: float32 [16384, 2048], P(('dp', 'tensor'))
- attn_gain_grad: float32 [2048], replicated
- query_weight_grad: float32 [2048, 2048], P('dp', 'tensor')
- key_weight_grad: float32 [2048, 2048], P('dp', 'tensor')
- value_weight_grad: float32 [2048, 2048], P('dp', 'tensor')
- out_weight_grad: float32 [2048, 2048], P('dp', 'tensor')
- mlp_gain_grad: float32 [2048], replicated
- gate_weight_grad: float32 [2048, 5504], P('dp', 'tensor')
- up_weight_grad: float32 [2048, 5504], P('dp', 'tensor')
- down_weight_grad: float32 [2048, 5504], P('dp', 'tensor')
Inputs may be any that keep to these rules, and one draw needn't show every extreme that they name: Each row holds the lengths of 8 sequences that fill one dp index's 1024 tokens in order; they sum to 1024 and the longest is exactly 512.
All inputs are finite; a program needn't handle non-finite values.
Results may differ from a plain program's by a relative error of at most 0.02.
Values may be sent and summed in bfloat16 or wider, within the bound.
A program may use at most 128 MiB of HBM per device.

v0:
```python
import jax
import jax.numpy as jnp
from jax import lax
from jax.sharding import PartitionSpec as P

HEAD_DIM = 128
QBLOCK = 512


EPS = 1e-05
THETA = 10000.0


def places(lengths_row, group_rows):
    seq_ends = jnp.cumsum(lengths_row)
    indices = jnp.arange(group_rows, dtype=jnp.int32)
    passed = indices[:, None] >= seq_ends[None, :]
    segment = jnp.sum(passed.astype(jnp.int32), axis=1)
    seq_start = jnp.sum(jnp.where(passed, lengths_row[None, :], 0), axis=1)
    return (segment, indices - seq_start)


def rotary(position, head_width):
    half_width = head_width // 2
    rates = THETA ** (-(jnp.arange(half_width, dtype=jnp.float32) * 2.0 / head_width))
    angles = position.astype(jnp.float32)[:, None] * rates[None, :]
    rot_cos = jnp.cos(angles)
    rot_sin = jnp.sin(angles)
    return (jnp.concatenate([rot_cos, rot_cos], 1), jnp.concatenate([rot_sin, rot_sin], 1))


def rotate(vector, rot_cos, rot_sin):
    half_width = vector.shape[-1] // 2
    turned = jnp.concatenate([-vector[..., half_width:], vector[..., :half_width]], -1)
    return vector * rot_cos[:, None, :] + turned * rot_sin[:, None, :]


def rotate_back(grad_rows, rot_cos, rot_sin):
    half_width = grad_rows.shape[-1] // 2
    moved = grad_rows * rot_sin[:, None, :]
    turned = jnp.concatenate([-moved[..., half_width:], moved[..., :half_width]], -1)
    return grad_rows * rot_cos[:, None, :] - turned


def scaled_norm(vector, gain_row):
    factor = lax.rsqrt(jnp.mean(vector * vector, axis=-1, keepdims=True) + EPS)
    return (vector * factor * gain_row, factor)


def norm_back(vector, factor, gain_row, grad_rows):
    inner = grad_rows * gain_row
    return factor * inner - vector * (factor * factor * factor) * jnp.mean(
        vector * inner, axis=-1, keepdims=True
    )


def contract(left, right):
    return lax.dot_general(
        left, right, (((1,), (1,)), ((), ())), preferred_element_type=jnp.float32
    )


def outer_sum(left, right):
    return lax.dot_general(
        left, right, (((0,), (0,)), ((), ())), preferred_element_type=jnp.float32
    )


def allowed_mask(segment, offset, block):
    group_rows = segment.shape[0]
    indices = jnp.arange(group_rows, dtype=jnp.int32)
    query_at = offset + jnp.arange(block, dtype=jnp.int32)
    seg_block = lax.dynamic_slice_in_dim(segment, offset, block, 0)
    return (seg_block[:, None] == segment[None, :]) & (indices[None, :] <= query_at[:, None])


def attention_forward(queries, key_rows, value_rows, segment, block):
    group_rows, head_count, head_width = queries.shape
    score_scale = head_width ** (-0.5)

    def one_block(offset):
        query_block = lax.dynamic_slice_in_dim(queries, offset, block, 0)
        allowed = allowed_mask(segment, offset, block)
        scores = (
            jnp.einsum("qhd,khd->hqk", query_block, key_rows, preferred_element_type=jnp.float32)
            * score_scale
        )
        scores = jnp.where(allowed[None], scores, -1e30)
        row_max = jnp.max(scores, axis=-1, keepdims=True)
        raised = jnp.exp(scores - row_max)
        totals = jnp.sum(raised, axis=-1, keepdims=True)
        weights = (raised / totals).astype(jnp.bfloat16)
        mixed_out = jnp.einsum(
            "hqk,khd->qhd", weights, value_rows, preferred_element_type=jnp.float32
        )
        return (mixed_out.astype(jnp.bfloat16), (row_max + jnp.log(totals))[..., 0])

    offsets = jnp.arange(group_rows // block, dtype=jnp.int32) * block
    mixed_out, log_totals = lax.map(one_block, offsets)
    return (mixed_out.reshape(group_rows, head_count * head_width), log_totals)


def attention_backward(queries, key_rows, value_rows, segment, log_totals, out_grad, block):
    group_rows, head_count, head_width = queries.shape
    score_scale = head_width ** (-0.5)

    def back_step(carried, block_in):
        key_grad, value_grad = carried
        offset, lse_block = block_in
        query_block = lax.dynamic_slice_in_dim(queries, offset, block, 0)
        grad_block = lax.dynamic_slice_in_dim(out_grad, offset, block, 0)
        allowed = allowed_mask(segment, offset, block)
        scores = (
            jnp.einsum("qhd,khd->hqk", query_block, key_rows, preferred_element_type=jnp.float32)
            * score_scale
        )
        scores = jnp.where(allowed[None], scores, -1e30)
        probs = jnp.exp(scores - lse_block[..., None])
        weights = probs.astype(jnp.bfloat16)
        value_grad = value_grad + jnp.einsum(
            "hqk,qhd->khd", weights, grad_block, preferred_element_type=jnp.float32
        )
        prob_grad = jnp.einsum(
            "qhd,khd->hqk", grad_block, value_rows, preferred_element_type=jnp.float32
        )
        centre = jnp.sum(probs * prob_grad, axis=-1, keepdims=True)
        score_grad = (probs * (prob_grad - centre)).astype(jnp.bfloat16)
        query_grad = (
            jnp.einsum("hqk,khd->qhd", score_grad, key_rows, preferred_element_type=jnp.float32)
            * score_scale
        )
        key_grad = (
            key_grad
            + jnp.einsum(
                "hqk,qhd->khd", score_grad, query_block, preferred_element_type=jnp.float32
            )
            * score_scale
        )
        return ((key_grad, value_grad), query_grad)

    offsets = jnp.arange(group_rows // block, dtype=jnp.int32) * block
    zeros_rows = jnp.zeros((group_rows, head_count, head_width), jnp.float32)
    (key_grad, value_grad), query_grad = lax.scan(
        back_step, (zeros_rows, zeros_rows), (offsets, log_totals)
    )
    return (query_grad.reshape(group_rows, head_count, head_width), key_grad, value_grad)


def shards(
    tokens,
    lengths,
    attn_gain,
    query_weight,
    key_weight,
    value_weight,
    out_weight,
    mlp_gain,
    gate_weight,
    up_weight,
    down_weight,
    cotangent,
):
    local_rows = tokens.shape[0]
    group_rows = local_rows * lax.axis_size("tensor")
    heads_here = query_weight.shape[1] // HEAD_DIM
    block = min(QBLOCK, group_rows)
    segment, position = places(lengths[0], group_rows)
    rot_cos, rot_sin = rotary(position, HEAD_DIM)
    shape_heads = (group_rows, heads_here, HEAD_DIM)
    residual = tokens.astype(jnp.float32)
    normed, factor_attn = scaled_norm(residual, attn_gain)
    normed_all = lax.all_gather(normed.astype(jnp.bfloat16), "tensor", axis=0, tiled=True)
    wq_full, wk_full, wv_full, wo_full = (
        lax.all_gather(query_weight, "dp", axis=0, tiled=True),
        lax.all_gather(key_weight, "dp", axis=0, tiled=True),
        lax.all_gather(value_weight, "dp", axis=0, tiled=True),
        lax.all_gather(out_weight, "dp", axis=0, tiled=True),
    )
    query_pre = jnp.dot(normed_all, wq_full, preferred_element_type=jnp.float32).reshape(
        shape_heads
    )
    key_pre = jnp.dot(normed_all, wk_full, preferred_element_type=jnp.float32).reshape(shape_heads)
    value_rows = (
        jnp.dot(normed_all, wv_full, preferred_element_type=jnp.float32)
        .astype(jnp.bfloat16)
        .reshape(shape_heads)
    )
    queries = rotate(query_pre, rot_cos, rot_sin).astype(jnp.bfloat16)
    key_rows = rotate(key_pre, rot_cos, rot_sin).astype(jnp.bfloat16)
    attended, log_totals = attention_forward(queries, key_rows, value_rows, segment, block)
    attn_branch = lax.psum_scatter(
        contract(attended, wo_full), "tensor", scatter_dimension=0, tiled=True
    )
    hidden_res = residual + attn_branch
    normed_two, factor_mlp = scaled_norm(hidden_res, mlp_gain)
    normed_two_all = lax.all_gather(normed_two.astype(jnp.bfloat16), "tensor", axis=0, tiled=True)
    wg_full, wu_full, wd_full = (
        lax.all_gather(gate_weight, "dp", axis=0, tiled=True),
        lax.all_gather(up_weight, "dp", axis=0, tiled=True),
        lax.all_gather(down_weight, "dp", axis=0, tiled=True),
    )
    gate = jnp.dot(normed_two_all, wg_full, preferred_element_type=jnp.float32)
    up_part = jnp.dot(normed_two_all, wu_full, preferred_element_type=jnp.float32)
    sigmoid_gate = jax.nn.sigmoid(gate)
    activated = gate * sigmoid_gate
    inner = (activated * up_part).astype(jnp.bfloat16)
    mlp_branch = lax.psum_scatter(
        contract(inner, wd_full).astype(jnp.bfloat16), "tensor", scatter_dimension=0, tiled=True
    ).astype(jnp.float32)
    output = (hidden_res + mlp_branch).astype(jnp.bfloat16)
    cotangent_all = lax.all_gather(cotangent, "tensor", axis=0, tiled=True)
    wg_back, wu_back, wd_back = (
        lax.all_gather(gate_weight, "dp", axis=0, tiled=True),
        lax.all_gather(up_weight, "dp", axis=0, tiled=True),
        lax.all_gather(down_weight, "dp", axis=0, tiled=True),
    )
    inner_grad = jnp.dot(cotangent_all, wd_back, preferred_element_type=jnp.float32)
    gate_grad = (inner_grad * up_part * sigmoid_gate * (1.0 + gate * (1.0 - sigmoid_gate))).astype(
        jnp.bfloat16
    )
    up_grad = (inner_grad * activated).astype(jnp.bfloat16)
    down_wgrad = outer_sum(cotangent_all, inner)
    gate_wgrad = outer_sum(normed_two_all, gate_grad)
    up_wgrad = outer_sum(normed_two_all, up_grad)
    normed_two_part = contract(gate_grad, wg_back) + contract(up_grad, wu_back)
    normed_two_grad = lax.psum_scatter(
        normed_two_part.astype(jnp.bfloat16), "tensor", scatter_dimension=0, tiled=True
    ).astype(jnp.float32)
    hidden_grad = cotangent.astype(jnp.float32) + norm_back(
        hidden_res, factor_mlp, mlp_gain, normed_two_grad
    )
    mlp_gain_part = jnp.sum(normed_two_grad * hidden_res * factor_mlp, axis=0)
    branch_all = lax.all_gather(hidden_grad.astype(jnp.bfloat16), "tensor", axis=0, tiled=True)
    wq_back, wk_back, wv_back, wo_back = (
        lax.all_gather(query_weight, "dp", axis=0, tiled=True),
        lax.all_gather(key_weight, "dp", axis=0, tiled=True),
        lax.all_gather(value_weight, "dp", axis=0, tiled=True),
        lax.all_gather(out_weight, "dp", axis=0, tiled=True),
    )
    attended_grad = (
        jnp.dot(branch_all, wo_back, preferred_element_type=jnp.float32)
        .astype(jnp.bfloat16)
        .reshape(shape_heads)
    )
    query_grad_rot, key_grad_rot, value_grad = attention_backward(
        queries, key_rows, value_rows, segment, log_totals, attended_grad, block
    )
    query_grad = (
        rotate_back(query_grad_rot, rot_cos, rot_sin).astype(jnp.bfloat16).reshape(group_rows, -1)
    )
    key_grad = (
        rotate_back(key_grad_rot, rot_cos, rot_sin).astype(jnp.bfloat16).reshape(group_rows, -1)
    )
    value_grad = value_grad.astype(jnp.bfloat16).reshape(group_rows, -1)
    out_wgrad = outer_sum(branch_all, attended)
    query_wgrad = outer_sum(normed_all, query_grad)
    key_wgrad = outer_sum(normed_all, key_grad)
    value_wgrad = outer_sum(normed_all, value_grad)
    normed_part = (
        contract(query_grad, wq_back) + contract(key_grad, wk_back) + contract(value_grad, wv_back)
    )
    normed_grad = lax.psum_scatter(
        normed_part.astype(jnp.bfloat16), "tensor", scatter_dimension=0, tiled=True
    ).astype(jnp.float32)
    tokens_grad = hidden_grad + norm_back(residual, factor_attn, attn_gain, normed_grad)
    attn_gain_part = jnp.sum(normed_grad * residual * factor_attn, axis=0)
    summed = (
        lax.psum_scatter(
            query_wgrad.astype(jnp.bfloat16), "dp", scatter_dimension=0, tiled=True
        ).astype(jnp.float32),
        lax.psum_scatter(
            key_wgrad.astype(jnp.bfloat16), "dp", scatter_dimension=0, tiled=True
        ).astype(jnp.float32),
        lax.psum_scatter(
            value_wgrad.astype(jnp.bfloat16), "dp", scatter_dimension=0, tiled=True
        ).astype(jnp.float32),
        lax.psum_scatter(
            out_wgrad.astype(jnp.bfloat16), "dp", scatter_dimension=0, tiled=True
        ).astype(jnp.float32),
        lax.psum_scatter(
            gate_wgrad.astype(jnp.bfloat16), "dp", scatter_dimension=0, tiled=True
        ).astype(jnp.float32),
        lax.psum_scatter(
            up_wgrad.astype(jnp.bfloat16), "dp", scatter_dimension=0, tiled=True
        ).astype(jnp.float32),
        lax.psum_scatter(
            down_wgrad.astype(jnp.bfloat16), "dp", scatter_dimension=0, tiled=True
        ).astype(jnp.float32),
    )
    gain_sums = lax.psum((attn_gain_part, mlp_gain_part), ("dp", "tensor"))
    return (
        output,
        tokens_grad,
        gain_sums[0],
        summed[0],
        summed[1],
        summed[2],
        summed[3],
        gain_sums[1],
        summed[4],
        summed[5],
        summed[6],
    )


def solution(mesh):
    return jax.shard_map(
        shards,
        mesh=mesh,
        in_specs=(
            P(("dp", "tensor"), None),
            P("dp", None),
            P(),
            P("dp", "tensor"),
            P("dp", "tensor"),
            P("dp", "tensor"),
            P("dp", "tensor"),
            P(),
            P("dp", "tensor"),
            P("dp", "tensor"),
            P("dp", "tensor"),
            P(("dp", "tensor"), None),
        ),
        out_specs=(
            P(("dp", "tensor"), None),
            P(("dp", "tensor"), None),
            P(),
            P("dp", "tensor"),
            P("dp", "tensor"),
            P("dp", "tensor"),
            P("dp", "tensor"),
            P(),
            P("dp", "tensor"),
            P("dp", "tensor"),
            P("dp", "tensor"),
        ),
        check_vma=False,
    )
```

profile of v0, /device:TPU:1, one launch (start us, length us, event | category | flops | bytes accessed | tf_op | source)
XLA Modules:
  0.0 1410.7 jit_solution(11075221460301784596)
XLA Ops:
  18.6 40.3 %all-gather.18.cloned.1.call-done = bf16[2048,256]{1,0:T(8,128)(2,1)} async-done(((bf16[128,256]{1,0:T(8,128)(2,1)}), bf16[2048,256]{1,0:T(8,128)(2,1)}) %all-gather.18.cloned.1.call-update) | async-done | bytes 1048592 | tf_op jit(solution)/shard_map/all_gather | solution.py:176
  58.9 53.4 %all-gather.12.cloned.1.call-done = bf16[1024,2048]{1,0:T(8,128)(2,1)} async-done(((bf16[128,2048]{1,0:T(8,128)(2,1)}), bf16[1024,2048]{1,0:T(8,128)(2,1)}) %all-gather.12.cloned.1.call-update) | async-done | bytes 4194320 | tf_op jit(solution)/shard_map/all_gather | solution.py:172
  112.3 3.8 convolution_convert_fusion.9
  116.3 42.3 %all-gather.16.cloned.1.call-done = bf16[2048,256]{1,0:T(8,128)(2,1)} async-done(((bf16[128,256]{1,0:T(8,128)(2,1)}), bf16[2048,256]{1,0:T(8,128)(2,1)}) %all-gather.16.cloned.1.call-update) | async-done | bytes 1048592 | tf_op jit(solution)/shard_map/all_gather | solution.py:175
  158.6 3.8 fusion.74
  162.7 41.8 %all-gather.14.cloned.1.call-done = bf16[2048,256]{1,0:T(8,128)(2,1)} async-done(((bf16[128,256]{1,0:T(8,128)(2,1)}), bf16[2048,256]{1,0:T(8,128)(2,1)}) %all-gather.14.cloned.1.call-update) | async-done | bytes 1048592 | tf_op jit(solution)/shard_map/all_gather | solution.py:174
  204.5 4.7 fusion.73
  214.2 18.4 %while.27 = (s32[]{:T(128)}, bf16[2,512,2,128]{3,2,1,0:T(2,128)(2,1)}, f32[2,2,512]{2,1,0:T(2,128)S(1)}, s32[2]{0:T(128)S(1)}, s32[1024]{0:T(1024)S(1)}, /*index...) while((s32[]{:T(128)}, ...), condition=%wide.region_7.8_spmd, body=%wide.region_4.7_spmd.sunk | while | flops 551157248 | bytes 21018864 | solution.py:99
  232.7 17.7 %all-gather.20.cloned.1.call-done = bf16[2048,256]{1,0:T(8,128)(2,1)} async-done(((bf16[128,256]{1,0:T(8,128)(2,1)}), bf16[2048,256]{1,0:T(8,128)(2,1)}) %all-gather.20.cloned.1.call-update) | async-done | bytes 1048592 | tf_op jit(solution)/shard_map/all_gather | solution.py:177
  250.4 6.0 fusion.68
  257.2 90.6 %reduce-scatter.18.cloned.1.call-done = f32[128,2048]{1,0:T(8,128)} async-done(((f32[1024,2048]{1,0:T(8,128)}), f32[128,2048]{1,0:T(8,128)}) %reduce-scatter.18.cloned.1.call-update) | async-done | bytes 1048592 | tf_op jit(solution)/shard_map/reduce_scatter | solution.py:191
  352.5 46.9 %all-gather.26.cloned.1.call-done = bf16[2048,688]{0,1:T(8,128)(2,1)} async-done(((bf16[128,688]{0,1:T(8,128)(2,1)}), bf16[2048,688]{0,1:T(8,128)(2,1)}) %all-gather.26.cloned.1.call-update) | async-done | bytes 2818064 | tf_op jit(solution)/shard_map/all_gather | solution.py:199
  399.4 52.5 %all-gather.22.cloned.1.call-done = bf16[1024,2048]{1,0:T(8,128)(2,1)} async-done(((bf16[128,2048]{1,0:T(8,128)(2,1)}), bf16[1024,2048]{1,0:T(8,128)(2,1)}) %all-gather.22.cloned.1.call-update) | async-done | bytes 4194320 | tf_op jit(solution)/shard_map/all_gather | solution.py:196
  451.9 7.8 fusion.76
  459.6 43.9 %all-gather.24.cloned.1.call-done = bf16[2048,688]{0,1:T(8,128)(2,1)} async-done(((bf16[128,688]{0,1:T(8,128)(2,1)}), bf16[2048,688]{0,1:T(8,128)(2,1)}) %all-gather.24.cloned.1.call-update) | async-done | bytes 2818064 | tf_op jit(solution)/shard_map/all_gather | solution.py:198
  503.5 7.7 fusion.75
  511.2 42.5 %all-gather.28.cloned.1.call-done = bf16[2048,688]{0,1:T(8,128)(2,1)} async-done(((bf16[128,688]{0,1:T(8,128)(2,1)}), bf16[2048,688]{0,1:T(8,128)(2,1)}) %all-gather.28.cloned.1.call-update) | async-done | bytes 2818064 | tf_op jit(solution)/shard_map/all_gather | solution.py:200
  553.7 51.9 %all-gather.30.cloned.1.call-done = bf16[1024,2048]{1,0:T(8,128)(2,1)} async-done(((bf16[128,2048]{1,0:T(8,128)(2,1)}), bf16[1024,2048]{1,0:T(8,128)(2,1)}) %all-gather.30.cloned.1.call-update) | async-done | bytes 4194320 | tf_op jit(solution)/shard_map/all_gather | solution.py:211
  605.6 10.1 multiply_convert_fusion.1
  615.7 3.5 fusion.77
  619.3 5.6 add_convert_fusion.1
  625.0 52.1 %reduce-scatter.22.cloned.1.call-done = bf16[128,2048]{1,0:T(8,128)(2,1)} async-done(((bf16[1024,2048]{1,0:T(8,128)(2,1)}), bf16[128,2048]{1,0:T(8,128)(2,1)}) %reduce-scatter.22.cloned.1.call-update) | async-done | bytes 524304 | tf_op jit(solution)/shard_map/reduce_scatter | solution.py:226
  678.4 2.2 fusion.72
  680.7 7.2 fusion.41
  688.0 4.7 copy.113
  692.7 7.3 convolution_convert_fusion.2
  700.0 4.6 copy.109
  704.7 7.3 convolution_convert_fusion.1
  712.0 4.7 copy.111
  716.8 15.5 %all-gather.32.cloned.1.call-done = bf16[1024,2048]{1,0:T(8,128)(2,1)} async-done(((bf16[128,2048]{1,0:T(8,128)(2,1)}), bf16[1024,2048]{1,0:T(8,128)(2,1)}) %all-gather.32.cloned.1.call-update) | async-done | bytes 4194320 | tf_op jit(solution)/shard_map/all_gather | solution.py:233
  732.3 4.7 convolution_convert_fusion.4
  737.5 4.6 convolution_convert_fusion.8
  742.1 25.4 %while.28 = (s32[]{:T(128)}, f32[1024,2,128]{0,2,1:T(8,128)S(1)}, f32[1024,2,128]{0,2,1:T(8,128)}, f32[2,512,2,128]{3,1,2,0:T(8,128)}, s32[2]{0:T(128)S(1)}, /*i...) while((s32[]{:T(128)}, f32[1024,2,128]{0,2,1:T(8,128)S(1)}, ...), condition=%wide.region_15.16_spmd.clone, body=%wide.region_13.15_spmd.clone.sunk | while | flops 1360920064 | bytes 61909388 | solution.py:143
  768.9 4.7 convolution_convert_fusion.5
  780.7 4.6 convolution_convert_fusion.6
  790.1 2.4 convolution_convert_fusion.7
  792.6 2.6 fusion.78
  796.6 3.4 add_convert_fusion
  800.1 7.8 convolution_convert_fusion
  810.8 76.2 %reduce-scatter.34.cloned.1.call-done = bf16[128,688]{1,0:T(8,128)(2,1)} async-done(((bf16[2048,688]{1,0:T(8,128)(2,1)}), bf16[128,688]{1,0:T(8,128)(2,1)}) %reduce-scatter.34.cloned.1.call-update) | async-done | bytes 176144
  888.9 76.2 %reduce-scatter.36.cloned.1.call-done = bf16[128,688]{1,0:T(8,128)(2,1)} async-done(((bf16[2048,688]{1,0:T(8,128)(2,1)}), bf16[128,688]{1,0:T(8,128)(2,1)}) %reduce-scatter.36.cloned.1.call-update) | async-done | bytes 176144
  967.0 66.7 %reduce-scatter.32.cloned.1.call-done = bf16[128,256]{1,0:T(8,128)(2,1)} async-done(((bf16[2048,256]{1,0:T(8,128)(2,1)}), bf16[128,256]{1,0:T(8,128)(2,1)}) %reduce-scatter.32.cloned.1.call-update) | async-done | bytes 65552 | tf_op jit(solution)/shard_map/reduce_scatter | solution.py:277
  1035.2 68.5 %reduce-scatter.30.cloned.1.call-done = bf16[128,256]{1,0:T(8,128)(2,1)} async-done(((bf16[2048,256]{1,0:T(8,128)(2,1)}), bf16[128,256]{1,0:T(8,128)(2,1)}) %reduce-scatter.30.cloned.1.call-update) | async-done | bytes 65552 | tf_op jit(solution)/shard_map/reduce_scatter | solution.py:274
  1105.2 68.2 %reduce-scatter.28.cloned.1.call-done = bf16[128,256]{1,0:T(8,128)(2,1)} async-done(((bf16[2048,256]{1,0:T(8,128)(2,1)}), bf16[128,256]{1,0:T(8,128)(2,1)}) %reduce-scatter.28.cloned.1.call-update) | async-done | bytes 65552 | tf_op jit(solution)/shard_map/reduce_scatter | solution.py:271
  1174.9 69.1 %reduce-scatter.26.cloned.1.call-done = bf16[128,256]{1,0:T(8,128)(2,1)} async-done(((bf16[2048,256]{1,0:T(8,128)(2,1)}), bf16[128,256]{1,0:T(8,128)(2,1)}) %reduce-scatter.26.cloned.1.call-update) | async-done | bytes 65552 | tf_op jit(solution)/shard_map/reduce_scatter | solution.py:268
  1245.5 55.2 %reduce-scatter.24.cloned.1.call-done = bf16[128,2048]{1,0:T(8,128)(2,1)} async-done(((bf16[1024,2048]{1,0:T(8,128)(2,1)}), bf16[128,2048]{1,0:T(8,128)(2,1)}) %reduce-scatter.24.cloned.1.call-update) | async-done | bytes 524304 | tf_op jit(solution)/shard_map/reduce_scatter | solution.py:262
  1302.0 98.7 %all-reduce = (f32[2048]{0:T(1024)}, f32[2048]{0:T(1024)}) all-reduce(f32[2048]{0:T(1024)S(1)} %get-tuple-element.251, f32[2048]{0:T(1024)S(1)} %get-tuple-element.249), channel_id=1, replica_groups=mesh['dp'=16,'tensor'=8] {'dp','tensor'}, use_global_device_ids=true, to_apply=%region_19.20 | all-reduce | flops 4096 | bytes 32768 | tf_op jit(solution)/shard_map/psum | solution.py:290
  1400.8 2.9 fusion.47
  (220 shorter events, 88.5 us)
Async XLA Ops:
  7.2 51.7 %all-gather.18.cloned.1.call-start = ((), (), s32[]{:S(2)}) async-start(), calls=%async_computation.14 | async-start | bytes 1114112 | tf_op jit(solution)/shard_map/all_gather | solution.py:176
  7.9 104.4 %all-gather.12.cloned.1.call-start = ((), (), s32[]{:S(2)}) async-start(), calls=%async_computation.11 | async-start | bytes 4718592 | tf_op jit(solution)/shard_map/all_gather | solution.py:172
  9.7 5.6 copy-start.26
  11.8 146.8 %all-gather.16.cloned.1.call-start = ((), (), s32[]{:S(2)}) async-start(), calls=%async_computation.13 | async-start | bytes 1114112 | tf_op jit(solution)/shard_map/all_gather | solution.py:175
  12.5 192.0 %all-gather.14.cloned.1.call-start = ((), (), s32[]{:S(2)}) async-start(), calls=%async_computation.12 | async-start | bytes 1114112 | tf_op jit(solution)/shard_map/all_gather | solution.py:174
  13.1 237.3 %all-gather.20.cloned.1.call-start = ((), (), s32[]{:S(2)}) async-start(), calls=%async_computation.15 | async-start | bytes 1114112 | tf_op jit(solution)/shard_map/all_gather | solution.py:177
  13.7 334.1 %reduce-scatter.18.cloned.1.call-start = ((), (), s32[]{:S(2)}) async-start(), calls=%async_computation.16 | async-start | bytes 9437184 | tf_op jit(solution)/shard_map/reduce_scatter | solution.py:191
  232.7 23.7 %copy-start = (bf16[1024,2,128]{2,0,1:T(8,128)(2,1)}, bf16[1024,2,128]{2,0,1:T(8,128)(2,1)S(1)}, u32[]{:S(2)}) copy-start(bf16[1024,2,128]{2,0,1:T(8,128)(2,1)S(1)} %get-tuple-element.551) | copy-start | bytes 1572868
  256.3 91.4 %copy-start.3 = (bf16[128,2048]{1,0:T(8,128)(2,1)S(1)}, bf16[128,2048]{1,0:T(8,128)(2,1)}, u32[]{:S(2)}) copy-start(bf16[128,2048]{1,0:T(8,128)(2,1)} %param.16) | copy-start | bytes 1572868
  256.3 92.9 %copy-start.24 = (f32[2048]{0:T(1024)S(1)}, f32[2048]{0:T(1024)}, u32[]{:S(2)}) copy-start(f32[2048]{0:T(1024)} %param.23) | copy-start | bytes 24580
  256.4 143.0 %all-gather.26.cloned.1.call-start = ((), (), s32[]{:S(2)}) async-start(), calls=%async_computation.19 | async-start | bytes 2994176 | tf_op jit(solution)/shard_map/all_gather | solution.py:199
  257.1 194.7 %all-gather.22.cloned.1.call-start = ((), (), s32[]{:S(2)}) async-start(), calls=%async_computation.17 | async-start | bytes 4718592 | tf_op jit(solution)/shard_map/all_gather | solution.py:196
  350.2 153.3 %all-gather.24.cloned.1.call-start = ((), (), s32[]{:S(2)}) async-start(), calls=%async_computation.18 | async-start | bytes 2994176 | tf_op jit(solution)/shard_map/all_gather | solution.py:198
  351.0 202.8 %all-gather.28.cloned.1.call-start = ((), (), s32[]{:S(2)}) async-start(), calls=%async_computation.20 | async-start | bytes 2994176 | tf_op jit(solution)/shard_map/all_gather | solution.py:200
  351.6 254.1 %all-gather.30.cloned.1.call-start = ((), (), s32[]{:S(2)}) async-start(), calls=%async_computation.22 | async-start | bytes 4718592 | tf_op jit(solution)/shard_map/all_gather | solution.py:211
  352.3 324.8 %reduce-scatter.22.cloned.1.call-start = ((), (), s32[]{:S(2)}) async-start(), calls=%async_computation.23 | async-start | bytes 4718592 | tf_op jit(solution)/shard_map/reduce_scatter | solution.py:226
  605.6 10.1 copy-start.31
  615.7 3.6 copy-start.32
  615.7 3.6 copy-start.33
  615.7 3.6 copy-start.30
  624.9 53.5 %copy-start.10 = (bf16[128,2048]{1,0:T(8,128)(2,1)S(1)}, bf16[128,2048]{1,0:T(8,128)(2,1)}, u32[]{:S(2)}) copy-start(bf16[128,2048]{1,0:T(8,128)(2,1)} %param.27) | copy-start | bytes 1572868
  624.9 107.3 %all-gather.32.cloned.1.call-start = ((), (), s32[]{:S(2)}) async-start(), calls=%async_computation.24 | async-start | bytes 4718592 | tf_op jit(solution)/shard_map/all_gather | solution.py:233
  680.7 128.3 %reduce-scatter.38.cloned.1.call-start = ((), (), s32[]{:S(2)}) async-start(), calls=%async_computation.32 | async-start | bytes 3342336
  692.7 194.4 %reduce-scatter.34.cloned.1.call-start = ((), (), s32[]{:S(2)}) async-start(), calls=%async_computation.30 | async-start | bytes 3342336
  704.7 260.5 %reduce-scatter.36.cloned.1.call-start = ((), (), s32[]{:S(2)}) async-start(), calls=%async_computation.31 | async-start | bytes 3342336
  716.7 317.0 %reduce-scatter.32.cloned.1.call-start = ((), (), s32[]{:S(2)}) async-start(), calls=%async_computation.29 | async-start | bytes 1114112 | tf_op jit(solution)/shard_map/reduce_scatter | solution.py:277
  737.0 366.7 %reduce-scatter.30.cloned.1.call-start = ((), (), s32[]{:S(2)}) async-start(), calls=%async_computation.28 | async-start | bytes 1114112 | tf_op jit(solution)/shard_map/reduce_scatter | solution.py:274
  744.6 2.2 copy-start.15
  744.6 2.2 copy-start.20
  748.5 2.0 copy-start.21
  757.3 2.2 copy-start.15
  757.3 2.2 copy-start.20
  761.2 2.0 copy-start.21
  768.9 4.7 copy-start.16
  773.6 2.7 copy-start.9
  773.7 399.7 %reduce-scatter.28.cloned.1.call-start = ((), (), s32[]{:S(2)}) async-start(), calls=%async_computation.27 | async-start | bytes 1114112 | tf_op jit(solution)/shard_map/reduce_scatter | solution.py:271
  776.3 1.9 copy-start.5
  785.3 458.7 %reduce-scatter.26.cloned.1.call-start = ((), (), s32[]{:S(2)}) async-start(), calls=%async_computation.26 | async-start | bytes 1114112 | tf_op jit(solution)/shard_map/reduce_scatter | solution.py:268
  787.9 2.2 copy-start.29
  792.5 2.7 copy-start.19
  792.5 508.1 %reduce-scatter.24.cloned.1.call-start = ((), (), s32[]{:S(2)}) async-start(), calls=%async_computation.25 | async-start | bytes 4718592 | tf_op jit(solution)/shard_map/reduce_scatter | solution.py:262
  800.0 600.7 %reduce-scatter.20.cloned.1.call-start = ((), (), s32[]{:S(2)}) async-start(), calls=%async_computation.21 | async-start | bytes 4718592 | tf_op jit(solution)/shard_map/reduce_scatter | solution.py:207
  807.9 492.8 %copy-start.4 = (bf16[128,2048]{1,0:T(8,128)(2,1)S(1)}, bf16[128,2048]{1,0:T(8,128)(2,1)}, u32[]{:S(2)}) copy-start(bf16[128,2048]{1,0:T(8,128)(2,1)} %param.16) | copy-start | bytes 1572868
  807.9 492.8 %copy-start.25 = (f32[2048]{0:T(1024)S(1)}, f32[2048]{0:T(1024)}, u32[]{:S(2)}) copy-start(f32[2048]{0:T(1024)} %param.18) | copy-start | bytes 24580
  807.9 492.8 %copy-start.27 = (f32[128]{0:T(128)S(1)}, f32[128]{0:T(128)}, u32[]{:S(2)}) copy-start(f32[128]{0:T(128)} %copy-done.26) | copy-start | bytes 1540
  807.9 592.9 %copy-start.11 = (bf16[128,2048]{1,0:T(8,128)(2,1)S(1)}, bf16[128,2048]{1,0:T(8,128)(2,1)}, u32[]{:S(2)}) copy-start(bf16[128,2048]{1,0:T(8,128)(2,1)} %param.27) | copy-start | bytes 1572868
  807.9 592.9 %copy-start.12 = (bf16[128,2048]{1,0:T(8,128)(2,1)S(1)}, bf16[128,2048]{1,0:T(8,128)(2,1)}, u32[]{:S(2)}) copy-start(bf16[128,2048]{1,0:T(8,128)(2,1)} %reduce-scatter.22.cloned.1.call-done) | copy-start | bytes 1572868
  807.9 592.9 %copy-start.28 = (f32[128]{0:T(128)S(1)}, f32[128]{0:T(128)}, u32[]{:S(2)}) copy-start(f32[128]{0:T(128)} %get-tuple-element.320) | copy-start | bytes 1540
  (16 other events, 21.4 us)
Sparse Core Ops, SparseCore 0:
  10.5 48.3 all-gather.17
  61.1 51.1 all-gather.11
  114.8 43.8 all-gather.15
  160.9 43.5 all-gather.13
  206.8 43.5 all-gather.19
  256.5 91.2 reduce-scatter.17
  350.1 49.2 all-gather.25
  401.6 50.2 all-gather.21
  454.2 49.2 all-gather.23
  505.7 48.0 all-gather.27
  555.4 50.2 all-gather.29
  625.0 51.9 reduce-scatter.21
  680.8 51.4 all-gather.31
  736.2 72.7 reduce-scatter.37
  812.9 74.1 reduce-scatter.33
  891.0 74.1 reduce-scatter.35
  968.8 64.9 reduce-scatter.31
  1037.8 65.8 reduce-scatter.29
  1107.5 65.8 reduce-scatter.27
  1178.0 65.8 reduce-scatter.25
  1246.4 54.2 reduce-scatter.23
  1303.1 52.4 reduce-scatter.19
where the time goes:
time: 1420 us; the launch traced here: 1410 us
  waiting for transfers between devices  1080 us (76%)
  matrix products  128 us (9%)
  blocking collectives  98.7 us (7%)
  other arithmetic  45.2 us (3%)
  local copies, waits for them, and re-layouts  36 us (3%)
  between operations  15 us (1%)
    unnamed x25, waiting for transfers between devices  159 us
    psum x1, blocking collectives, shards(): gain_sums = lax.psum((attn_gain_part, mlp_gain_part), ('dp', 'tensor'))  98.7 us
    reduce_scatter x1, waiting for transfers between devices, shards(): lax.psum_scatter(contract(attended, wo_full), 'tensor', scatter_dimension...  90.6 us
    reduce_scatter x1, waiting for transfers between devices, shards(): lax.psum_scatter(query_wgrad.astype(jnp.bfloat16), 'dp', scatter_dimensio...  69.1 us
    reduce_scatter x1, waiting for transfers between devices, shards(): lax.psum_scatter(value_wgrad.astype(jnp.bfloat16), 'dp', scatter_dimensio...  68.5 us
    reduce_scatter x1, waiting for transfers between devices, shards(): lax.psum_scatter(key_wgrad.astype(jnp.bfloat16), 'dp', scatter_dimension=...  68.2 us
    reduce_scatter x1, waiting for transfers between devices, shards(): lax.psum_scatter(out_wgrad.astype(jnp.bfloat16), 'dp', scatter_dimension=...  66.7 us
    reduce_scatter x1, waiting for transfers between devices, shards(): lax.psum_scatter(normed_part.astype(jnp.bfloat16), 'tensor', scatter_dime...  55.2 us
  transfers between devices with their start and end apart: 22, of which 21 were waited for; matrix products, arithmetic and copies ran while one was open for 12% of the time, Pallas kernels for 0%

commit v1 on v0

--- a/solution.py
+++ b/solution.py
@@ -1,14 +1,638 @@
+import functools
+
 import jax
 import jax.numpy as jnp
 from jax import lax
+from jax.experimental import pallas as pl
+from jax.experimental.pallas import tpu as pltpu
 from jax.sharding import PartitionSpec as P
 
 HEAD_DIM = 128
 QBLOCK = 512
-
-
 EPS = 1e-05
 THETA = 10000.0
+D = 2048
+ROWS = 128
+GROUP = 1024
+FFB = 688
+CUT = 352
+MESH = pl.DeviceIdType.MESH
+ANY = pl.BlockSpec(memory_space=pl.ANY)
+VMEM = pl.BlockSpec(memory_space=pltpu.VMEM)
+
+
+class Net:
+    def __init__(self, send_sems, recv_sems):
+        dp, t = lax.axis_index("dp"), lax.axis_index("tensor")
+        self.y, self.c = lax.div(dp, 4), lax.rem(dp, 2)
+        self.xl, self.z = lax.div(t, 4), lax.rem(t, 4)
+        self.x = lax.rem(lax.div(dp, 2), 2) * 2 + self.xl
+        self.dp, self.t = dp, t
+        self.send_sems, self.recv_sems = send_sems, recv_sems
+        self.used = 0
+        self.sent = []
+
+    def device(self, dx=0, dy=0, dz=0, dc=0):
+        x, y = lax.rem(self.x + dx + 4, 4), lax.rem(self.y + dy + 4, 4)
+        z, c = lax.rem(self.z + dz + 4, 4), lax.rem(self.c + dc, 2)
+        return (y * 4 + lax.div(x, 2) * 2 + c, lax.rem(x, 2) * 4 + z)
+
+    @property
+    def beside(self):
+        return (self.dp, (1 - self.xl) * 4 + self.z)
+
+    @property
+    def across(self):
+        return self.device(dx=2)
+
+    def along(self, first):
+        on_x = self.c == (0 if first else 1)
+        both = []
+        for step in (1, -1):
+            by_x, by_y = self.device(dx=step), self.device(dy=step)
+            both.append(tuple(jnp.where(on_x, u, v) for u, v in zip(by_x, by_y)))
+        return both
+
+    def send(self, src, dst, to):
+        k = self.used
+        self.used += 1
+        copy = pltpu.make_async_remote_copy(
+            src_ref=src,
+            dst_ref=dst,
+            send_sem=self.send_sems.at[k],
+            recv_sem=self.recv_sems.at[k],
+            device_id=to,
+            device_id_type=MESH,
+        )
+        copy.start()
+        self.sent.append(copy)
+        return copy
+
+    def finish(self):
+        for copy in self.sent:
+            copy.wait_send()
+
+    def greet(self, devices):
+        barrier = pltpu.get_barrier_semaphore()
+        for device in devices:
+            pl.semaphore_signal(barrier, inc=1, device_id=device, device_id_type=MESH)
+        pl.semaphore_wait(barrier, len(devices))
+
+
+def take_turns(chains, order):
+    for name in order:
+        next(chains[name], None)
+    for chain in chains.values():
+        for _ in chain:
+            pass
+
+
+def block(z):
+    return pl.ds(pl.multiple_of(lax.rem(z + 8, 4) * ROWS, ROWS), ROWS)
+
+
+def half(z, k):
+    return pl.ds(pl.multiple_of(lax.rem(z + 8, 4) * ROWS + k * 64, 64), 64)
+
+
+def block8(xl, z):
+    return pl.ds(pl.multiple_of((xl * 4 + lax.rem(z + 8, 4)) * ROWS, ROWS), ROWS)
+
+
+def half8(xl, z, k):
+    return pl.ds(pl.multiple_of((xl * 4 + lax.rem(z + 8, 4)) * ROWS + k * 64, 64), 64)
+
+
+def add_rows(rows, dst, *terms):
+    def step(i, _):
+        at = pl.ds(pl.multiple_of(i * 16, 16), 16)
+        total = terms[0][at, :].astype(jnp.float32)
+        for term in terms[1:]:
+            total = total + term[at, :].astype(jnp.float32)
+        dst[at, :] = total.astype(dst.dtype)
+        return 0
+
+    lax.fori_loop(0, rows // 16, step, 0)
+
+
+def gather_z(net, own, dst):
+    up, down = net.device(dz=1), net.device(dz=-1)
+    z = net.z
+    a0 = net.send(own, dst.at[block(z), :], up)
+    a1 = net.send(own, dst.at[block(z), :], down)
+    yield
+    a0.wait_recv()
+    b0 = net.send(dst.at[half(z - 1, 0), :], dst.at[half(z - 1, 0), :], up)
+    a1.wait_recv()
+    b1 = net.send(dst.at[half(z + 1, 1), :], dst.at[half(z + 1, 1), :], down)
+    yield
+    b0.wait_recv()
+    b1.wait_recv()
+
+
+def gather_8(net, own, dst):
+    up, down, beside = net.device(dz=1), net.device(dz=-1), net.beside
+    xl, z = net.xl, net.z
+    place = dst.at[block8(xl, z), :]
+    s0 = net.send(own, place, up)
+    s1 = net.send(own, place, down)
+    s2 = net.send(own, place, beside)
+    yield
+    s0.wait_recv()
+    ref = dst.at[half8(xl, z - 1, 0), :]
+    s5 = net.send(ref, ref, up)
+    s1.wait_recv()
+    ref = dst.at[half8(xl, z + 1, 1), :]
+    s6 = net.send(ref, ref, down)
+    s2.wait_recv()
+    ref = dst.at[block8(1 - xl, z), :]
+    s3 = net.send(ref, ref, up)
+    s4 = net.send(ref, ref, down)
+    yield
+    s5.wait_recv()
+    s6.wait_recv()
+    ref = dst.at[block8(xl, z + 2), :]
+    s7 = net.send(ref, ref, beside)
+    yield
+    s3.wait_recv()
+    s4.wait_recv()
+    s7.wait_recv()
+
+
+def reduce_z(net, part, sums, got, out):
+    up, down = net.device(dz=1), net.device(dz=-1)
+    z = net.z
+    c0 = net.send(part.at[half(z + 2, 0), :], got.at[0], up)
+    c1 = net.send(part.at[half(z + 2, 1), :], got.at[1], down)
+    d1 = net.send(part.at[half(z + 1, 1), :], got.at[3], up)
+    d2 = net.send(part.at[half(z - 1, 0), :], got.at[4], down)
+    yield
+    c0.wait_recv()
+    add_rows(64, sums.at[0], part.at[half(z + 1, 0), :], got.at[0])
+    d0 = net.send(sums.at[0], got.at[2], up)
+    c1.wait_recv()
+    add_rows(64, sums.at[1], part.at[half(z - 1, 1), :], got.at[1])
+    d3 = net.send(sums.at[1], got.at[5], down)
+    yield
+    for copy in (d0, d1, d2, d3):
+        copy.wait_recv()
+    out.append(lambda at, k: part[pl.ds(pl.multiple_of(net.z * ROWS + at, 16), 16), :].astype(jnp.float32)
+               + got[2 + k, pl.ds(pl.multiple_of(at - 64 * k, 16), 16), :].astype(jnp.float32)
+               + got[4 + k, pl.ds(pl.multiple_of(at - 64 * k, 16), 16), :].astype(jnp.float32))
+
+
+def reduce_8(net, part, sums, got, sums_half, got_half, out):
+    up, down, beside = net.device(dz=1), net.device(dz=-1), net.beside
+    xl, z = net.xl, net.z
+    a = net.send(part.at[block8(1 - xl, z + 2), :], got.at[0], beside)
+    b0 = net.send(part.at[block8(1 - xl, z + 1), :], got.at[1], up)
+    b1 = net.send(part.at[block8(1 - xl, z - 1), :], got.at[2], down)
+    d1 = net.send(part.at[half8(xl, z + 1, 1), :], got_half.at[3], up)
+    d2 = net.send(part.at[half8(xl, z - 1, 0), :], got_half.at[4], down)
+    yield
+    a.wait_recv()
+    add_rows(128, sums.at[0], part.at[block8(xl, z + 2), :], got.at[0])
+    c0 = net.send(sums.at[0, pl.ds(0, 64), :], got_half.at[0], up)
+    c1 = net.send(sums.at[0, pl.ds(64, 64), :], got_half.at[1], down)
+    yield
+    b0.wait_recv()
+    b1.wait_recv()
+    add_rows(128, sums.at[1], part.at[block8(1 - xl, z), :], got.at[1], got.at[2])
+    e = net.send(sums.at[1], got.at[3], beside)
+    yield
+    c0.wait_recv()
+    add_rows(64, sums_half.at[0], part.at[half8(xl, z + 1, 0), :], got_half.at[0])
+    d0 = net.send(sums_half.at[0], got_half.at[2], up)
+    c1.wait_recv()
+    add_rows(64, sums_half.at[1], part.at[half8(xl, z - 1, 1), :], got_half.at[1])
+    d3 = net.send(sums_half.at[1], got_half.at[5], down)
+    yield
+    for copy in (e, d0, d1, d2, d3):
+        copy.wait_recv()
+
+    def rows(at, k):
+        here = pl.ds(pl.multiple_of(at - 64 * k, 16), 16)
+        total = part[pl.ds(pl.multiple_of(net.t * ROWS + at, 16), 16), :].astype(jnp.float32)
+        total = total + got[3, pl.ds(pl.multiple_of(at, 16), 16), :].astype(jnp.float32)
+        return total + got_half[2 + k, here, :].astype(jnp.float32) + got_half[4 + k, here, :].astype(jnp.float32)
+
+    out.append(rows)
+
+
+def each_half(step):
+    for k in (0, 1):
+        def body(i, _, k=k):
+            step(pl.multiple_of(k * 64 + i * 16, 16), k)
+            return 0
+
+        lax.fori_loop(0, 4, body, 0)
+
+
+def gather_plane(net, slab, cut, first, second):
+    low, high = cut
+    sib = net.device(dc=1)
+    second_up, second_down = second
+
+    def share(i, j):
+        ref = slab(i, j)
+        return net.send(ref, ref, sib)
+
+    def go(i):
+        ref = slab(i, 0)
+        return net.send(ref, ref, second_up), net.send(ref, ref, second_down)
+
+    shared = []
+    own = slab(0, 0)
+    ring = len(first) == 2
+    if ring:
+        a0, a1 = net.send(own, own, first[0]), net.send(own, own, first[1])
+    else:
+        a0 = net.send(own, own, first[0])
+    sent = {0: go(0)}
+    shared.append(share(0, 0))
+    yield
+    if ring:
+        a0.wait_recv()
+        ref = low(slab(-1, 0))
+        f0 = net.send(ref, ref, first[0])
+        a1.wait_recv()
+        ref = high(slab(1, 0))
+        f1 = net.send(ref, ref, first[1])
+        for i in (-1, 1):
+            sent[i] = go(i)
+            shared.append(share(i, 0))
+        yield
+        f0.wait_recv()
+        f1.wait_recv()
+        sent[2] = go(2)
+        shared.append(share(2, 0))
+    else:
+        a0.wait_recv()
+        sent[1] = go(1)
+        shared.append(share(1, 0))
+    halves = {}
+    for i in sent:
+        yield
+        sent[i][0].wait_recv()
+        ref = low(slab(i, -1))
+        h0 = net.send(ref, ref, second_up)
+        shared.append(share(i, -1))
+        sent[i][1].wait_recv()
+        ref = high(slab(i, 1))
+        h1 = net.send(ref, ref, second_down)
+        shared.append(share(i, 1))
+        halves[i] = (h0, h1)
+    for i in sent:
+        yield
+        halves[i][0].wait_recv()
+        halves[i][1].wait_recv()
+        shared.append(share(i, 2))
+    yield
+    for copy in shared:
+        copy.wait_recv()
+
+
+def reduce_plane(net, mine, other, from_sib, got_half, got_up, got_down, last_bufs, cut, add, first, second):
+    low, high = cut
+    sib = net.device(dc=1)
+    up, down = second
+    ring = len(first) == 2
+    steps = (0, 1, 3, 2) if ring else (0, 1)
+    shared = {}
+    for j in (2, 1, 3, 0):
+        for i in steps:
+            shared[i, j] = net.send(other(i, j), from_sib(i, j), sib)
+    yield
+    halves, full = {}, {}
+    for i in steps:
+        shared[i, 2].wait_recv()
+        add(None, mine(i, 2), from_sib(i, 2))
+        halves[i] = (
+            net.send(low(mine(i, 2)), low(got_half(i)), up),
+            net.send(high(mine(i, 2)), high(got_half(i)), down),
+        )
+        yield
+    for i in steps:
+        for j in (1, 3):
+            shared[i, j].wait_recv()
+            add(None, mine(i, j), from_sib(i, j))
+        halves[i][0].wait_recv()
+        add(0, mine(i, 1), got_half(i))
+        u = net.send(mine(i, 1), got_up(i), up)
+        halves[i][1].wait_recv()
+        add(1, mine(i, 3), got_half(i))
+        full[i] = (u, net.send(mine(i, 3), got_down(i), down))
+        yield
+    last = {}
+    for i in reversed(steps):
+        shared[i, 0].wait_recv()
+        full[i][0].wait_recv()
+        full[i][1].wait_recv()
+        add(None, mine(i, 0), from_sib(i, 0), got_up(i), got_down(i))
+        if ring and i == 2:
+            ref, to = mine(2, 0), last_bufs(2)
+            last[2] = (net.send(low(ref), low(to), first[0]), net.send(high(ref), high(to), first[1]))
+        if ring and i == 3:
+            last[2][1].wait_recv()
+            add(1, mine(3, 0), last_bufs(2))
+            last[3] = net.send(mine(3, 0), last_bufs(1), first[1])
+        if ring and i == 1:
+            last[2][0].wait_recv()
+            add(0, mine(1, 0), last_bufs(2))
+        if i == 1:
+            last[1] = net.send(mine(1, 0), last_bufs(0), first[0])
+        yield
+    last[1].wait_recv()
+    if ring:
+        last[3].wait_recv()
+        add(None, mine(0, 0), last_bufs(0), last_bufs(1))
+    else:
+        add(None, mine(0, 0), last_bufs(0))
+
+
+PIECES = {None: ((0, 176), (176, 176), (352, 176), (528, 160)), 0: ((0, 176), (176, 176)), 1: ((352, 176), (528, 160))}
+
+
+def add_slab(part, dst, *terms):
+    def step(m, _):
+        for at, n in PIECES[part]:
+            total = dst[m, at : at + n, :].astype(jnp.float32)
+            for term in terms:
+                total = total + term[m, at : at + n, :].astype(jnp.float32)
+            dst[m, at : at + n, :] = total.astype(dst.dtype)
+        return 0
+
+    lax.fori_loop(0, 3, step, 0)
+
+
+FF_CUT = (lambda ref: ref.at[:, pl.ds(0, CUT), :], lambda ref: ref.at[:, pl.ds(CUT, FFB - CUT), :])
+
+
+def ff_slab(net, ref, kind, i, j):
+    x = lax.rem(net.x + jnp.where(kind == 0, i, j) + 4, 4)
+    y = lax.rem(net.y + jnp.where(kind == 0, j, i) + 4, 4)
+    at = pl.ds(pl.multiple_of((y * 4 + lax.div(x, 2) * 2 + kind) * 128, 128), 128)
+    return ref.at[:, lax.rem(x, 2), :, at]
+
+
+def mlp_in_kernel(a_part, tok, gain, wg, wu, wd, w_all, n2_all, h1, n2, sums, got, sums_half, got_half, send_sems, recv_sems, sems):
+    net = Net(send_sems, recv_sems)
+    xy = [net.device(dx=1), net.device(dx=-1), net.device(dy=1), net.device(dy=-1)]
+    own = ff_slab(net, w_all, net.c, 0, 0)
+    copies = [pltpu.make_async_copy(w, own.at[k], sems.at[k]) for k, w in enumerate((wg, wu, wd))]
+    for copy in copies:
+        copy.start()
+    net.greet(xy + [net.device(dz=1), net.device(dz=-1), net.device(dc=1)])
+
+    def tokens():
+        out = []
+        yield from reduce_8(net, a_part, sums, got, sums_half, got_half, out)
+
+        def step(at, k):
+            here = pl.ds(at, 16)
+            h = tok[here, :].astype(jnp.float32) + out[0](at, k)
+            h1[here, :] = h
+            r = lax.rsqrt(jnp.mean(h * h, axis=-1, keepdims=True) + EPS)
+            n2[here, :] = (h * r * gain[...]).astype(jnp.bfloat16)
+
+        each_half(step)
+        place = pltpu.make_async_copy(n2, n2_all.at[block(net.z), :], sems.at[3])
+        place.start()
+        yield from gather_z(net, n2, n2_all)
+        place.wait()
+
+    def weights():
+        for copy in copies:
+            copy.wait()
+        slab = functools.partial(ff_slab, net, w_all, net.c)
+        yield from gather_plane(net, slab, FF_CUT, net.along(True), net.along(False))
+
+    take_turns({"t": tokens(), "w": weights()}, "twwttwtwtwwtwwww")
+    net.finish()
+
+
+def mlp_in(a_part, tok, gain, wg, wu, wd):
+    return pl.pallas_call(
+        mlp_in_kernel,
+        name="mlp_in",
+        out_shape=(
+            jax.ShapeDtypeStruct((3, 2, FFB, D), jnp.bfloat16),
+            jax.ShapeDtypeStruct((4 * ROWS, D), jnp.bfloat16),
+            jax.ShapeDtypeStruct((ROWS, D), jnp.float32),
+        ),
+        in_specs=[VMEM, VMEM, VMEM, ANY, ANY, ANY],
+        out_specs=(ANY, ANY, VMEM),
+        scratch_shapes=[
+            pltpu.VMEM((ROWS, D), jnp.bfloat16),
+            pltpu.VMEM((2, ROWS, D), jnp.bfloat16),
+            pltpu.VMEM((4, ROWS, D), jnp.bfloat16),
+            pltpu.VMEM((2, 64, D), jnp.bfloat16),
+            pltpu.VMEM((6, 64, D), jnp.bfloat16),
+            pltpu.SemaphoreType.DMA((64,)),
+            pltpu.SemaphoreType.DMA((64,)),
+            pltpu.SemaphoreType.DMA((4,)),
+        ],
+        compiler_params=pltpu.CompilerParams(collective_id=1, has_side_effects=True, vmem_limit_bytes=56 << 20),
+    )(a_part, tok, gain, wg, wu, wd)
+
+
+NT = (((1,), (1,)), ((), ()))
+TILES = ((0, 256), (256, 256), (512, 176))
+
+
+def mlp_kernel(w_all, n2_all, g_all, m_out, dn_out, grads, w, n2, g, hid, dgate, dup, turned, stage, sems, out_sems):
+    copies = [
+        pltpu.make_async_copy(n2_all, n2, sems.at[0]),
+        pltpu.make_async_copy(g_all, g, sems.at[1]),
+    ]
+    loads = [pltpu.make_async_copy(w_all.at[m, b], w.at[m, b], sems.at[2 + m * 2 + b]) for m in range(3) for b in range(2)]
+    for copy in copies + loads:
+        copy.start()
+    for copy in copies + loads:
+        copy.wait()
+
+    def ahead(b, _):
+        for at, n in TILES:
+            gate = lax.dot_general(n2[...], w[0, b, at : at + n, :], NT, preferred_element_type=jnp.float32)
+            up = lax.dot_general(n2[...], w[1, b, at : at + n, :], NT, preferred_element_type=jnp.float32)
+            dh = lax.dot_general(g[...], w[2, b, at : at + n, :], NT, preferred_element_type=jnp.float32)
+            sig = jax.nn.sigmoid(gate)
+            act = gate * sig
+            for k, (dst, value) in enumerate(
+                ((dgate, dh * up * sig * (1.0 + gate * (1.0 - sig))), (dup, dh * act), (hid, act * up))
+            ):
+                value = value.astype(jnp.bfloat16)
+                dst[b, :, at : at + n] = value
+                turned[k, b, at : at + n, :] = value.T
+        return 0
+
+    lax.fori_loop(0, 2, ahead, 0)
+
+    def back(i, _):
+        at = pl.ds(pl.multiple_of(i * 256, 256), 256)
+        m = jnp.dot(hid[0], w[2, 0, :, at], preferred_element_type=jnp.float32)
+        m = m + jnp.dot(hid[1], w[2, 1, :, at], preferred_element_type=jnp.float32)
+        m_out[:, at] = m.astype(jnp.bfloat16)
+        d = jnp.dot(dgate[0], w[0, 0, :, at], preferred_element_type=jnp.float32)
+        d = d + jnp.dot(dgate[1], w[0, 1, :, at], preferred_element_type=jnp.float32)
+        d = d + jnp.dot(dup[0], w[1, 0, :, at], preferred_element_type=jnp.float32)
+        d = d + jnp.dot(dup[1], w[1, 1, :, at], preferred_element_type=jnp.float32)
+        dn_out[:, at] = d.astype(jnp.bfloat16)
+        return 0
+
+    lax.fori_loop(0, 8, back, 0)
+
+    def put(i, m, b, slot):
+        at = pl.ds(pl.multiple_of(i * 256, 256), 256)
+        return pltpu.make_async_copy(stage.at[slot], grads.at[m, b, :, at], out_sems.at[slot])
+
+    def outer(i, _):
+        at = pl.ds(pl.multiple_of(i * 256, 256), 256)
+        for m in range(3):
+            right = (n2, n2, g)[m][:, at]
+            for b in range(2):
+                slot = m * 2 + b
+                pl.when(i > 0)(lambda: put(i - 1, m, b, slot).wait())
+                stage[slot] = jnp.dot(turned[m, b], right, preferred_element_type=jnp.float32).astype(jnp.bfloat16)
+                put(i, m, b, slot).start()
+        return 0
+
+    lax.fori_loop(0, 8, outer, 0)
+    for m in range(3):
+        for b in range(2):
+            put(7, m, b, m * 2 + b).wait()
+
+
+def mlp(w_all, n2_all, g_all):
+    bf = jnp.bfloat16
+    return pl.pallas_call(
+        mlp_kernel,
+        name="mlp",
+        out_shape=(
+            jax.ShapeDtypeStruct((512, D), bf),
+            jax.ShapeDtypeStruct((512, D), bf),
+            jax.ShapeDtypeStruct((3, 2, FFB, D), bf),
+        ),
+        in_specs=[ANY] * 3,
+        out_specs=(VMEM, VMEM, ANY),
+        scratch_shapes=[
+            pltpu.VMEM((3, 2, FFB, D), bf),
+            pltpu.VMEM((512, D), bf),
+            pltpu.VMEM((512, D), bf),
+            pltpu.VMEM((2, 512, FFB), bf),
+            pltpu.VMEM((2, 512, FFB), bf),
+            pltpu.VMEM((2, 512, FFB), bf),
+            pltpu.VMEM((3, 2, FFB, 512), bf),
+            pltpu.VMEM((6, FFB, 256), bf),
+            pltpu.SemaphoreType.DMA((8,)),
+            pltpu.SemaphoreType.DMA((6,)),
+        ],
+        compiler_params=pltpu.CompilerParams(vmem_limit_bytes=58 << 20),
+        cost_estimate=pl.CostEstimate(flops=26 * 10**9, bytes_accessed=40 << 20, transcendentals=704512),
+    )(w_all, n2_all, g_all)
+
+
+def mlp_out_kernel(m_part, dn_part, grads, h1, gain, cot, mixed, dh1, da_all, gain_part, wg, wu, wd,
+                   da, sums_m, got_m, sums_d, got_d, mine, sib, got_half, got_up, got_down, last, send_sems, recv_sems, sems):
+    net = Net(send_sems, recv_sems)
+    xy = [net.device(dx=1), net.device(dx=-1), net.device(dy=1), net.device(dy=-1)]
+    order = [(i, j) for j in (2, 1, 3, 0) for i in (0, 1, 3, 2)]
+    loads = {}
+    for k, (i, j) in enumerate(order):
+        loads[i, j] = pltpu.make_async_copy(ff_slab(net, grads, net.c, i, j), mine.at[i, j], sems.at[k])
+        loads[i, j].start()
+    net.greet(xy + [net.device(dz=1), net.device(dz=-1), net.device(dc=1)])
+
+    def tokens():
+        out = []
+        yield from reduce_z(net, dn_part, sums_d, got_d, out)
+
+        def step(at, k, total):
+            here = pl.ds(at, 16)
+            h = h1[here, :]
+            r = lax.rsqrt(jnp.mean(h * h, axis=-1, keepdims=True) + EPS)
+            d = out[0](at, k)
+            inner = d * gain[...]
+            grad = r * inner - h * (r * r * r) * jnp.mean(h * inner, axis=-1, keepdims=True)
+            grad = cot[here, :].astype(jnp.float32) + grad
+            dh1[here, :] = grad
+            da[here, :] = grad.astype(jnp.bfloat16)
+            gain_part[...] += jnp.sum(d * h * r, axis=0, keepdims=True)
+
+        gain_part[...] = jnp.zeros_like(gain_part)
+        each_half(lambda at, k: step(at, k, None))
+        place = pltpu.make_async_copy(da, da_all.at[block8(net.xl, net.z), :], sems.at[16])
+        place.start()
+        yield from gather_8(net, da, da_all)
+        place.wait()
+
+    def forward():
+        out = []
+        yield from reduce_z(net, m_part, sums_m, got_m, out)
+
+        def step(at, k):
+            here = pl.ds(at, 16)
+            mixed[here, :] = (h1[here, :] + out[0](at, k)).astype(jnp.bfloat16)
+
+        each_half(step)
+
+    def weights():
+        waited = set()
+
+        def add(part, dst, *terms):
+            add_slab(part, dst, *terms)
+
+        def slot(ref):
+            return lambda i, j: ref.at[i, j]
+
+        sib_kind = 1 - net.c
+        for copy in loads.values():
+            copy.wait()
+        yield from reduce_plane(
+            net, slot(mine), functools.partial(ff_slab, net, grads, sib_kind), slot(sib),
+            lambda i: got_half.at[i], lambda i: got_up.at[i], lambda i: got_down.at[i], lambda i: last.at[i],
+            FF_CUT, add, net.along(True), net.along(False),
+        )
+        for k, dst in enumerate((wg, wu, wd)):
+            for at, n in PIECES[None]:
+                dst[at : at + n, :] = mine[0, 0, k, at : at + n, :].astype(jnp.float32)
+
+    take_turns({"t": tokens(), "m": forward(), "w": weights()}, "twwwwtwmwwtwwtwwtwww")
+    net.finish()
+
+
+def mlp_out(m_part, dn_part, grads, h1, gain, cot):
+    bf, f32 = jnp.bfloat16, jnp.float32
+    slab = (3, FFB, 128)
+    return pl.pallas_call(
+        mlp_out_kernel,
+        name="mlp_out",
+        out_shape=(
+            jax.ShapeDtypeStruct((ROWS, D), bf),
+            jax.ShapeDtypeStruct((ROWS, D), f32),
+            jax.ShapeDtypeStruct((GROUP, D), bf),
+            jax.ShapeDtypeStruct((1, D), f32),
+        ) + (jax.ShapeDtypeStruct((FFB, 128), f32),) * 3,
+        in_specs=[VMEM, VMEM, ANY, VMEM, VMEM, VMEM],
+        out_specs=(VMEM, VMEM, ANY, VMEM, VMEM, VMEM, VMEM),
+        scratch_shapes=[
+            pltpu.VMEM((ROWS, D), bf),
+            pltpu.VMEM((2, 64, D), bf),
+            pltpu.VMEM((6, 64, D), bf),
+            pltpu.VMEM((2, 64, D), bf),
+            pltpu.VMEM((6, 64, D), bf),
+            pltpu.VMEM((4, 4) + slab, bf),
+            pltpu.VMEM((4, 4) + slab, bf),
+            pltpu.VMEM((4,) + slab, bf),
+            pltpu.VMEM((4,) + slab, bf),
+            pltpu.VMEM((4,) + slab, bf),
+            pltpu.VMEM((3,) + slab, bf),
+            pltpu.SemaphoreType.DMA((64,)),
+            pltpu.SemaphoreType.DMA((64,)),
+            pltpu.SemaphoreType.DMA((17,)),
+        ],
+        compiler_params=pltpu.CompilerParams(collective_id=2, has_side_effects=True, vmem_limit_bytes=56 << 20),
+    )(m_part, dn_part, grads, h1, gain, cot)
 
 
 def places(lengths_row, group_rows):
@@ -188,49 +812,15 @@
     queries = rotate(query_pre, rot_cos, rot_sin).astype(jnp.bfloat16)
     key_rows = rotate(key_pre, rot_cos, rot_sin).astype(jnp.bfloat16)
     attended, log_totals = attention_forward(queries, key_rows, value_rows, segment, block)
-    attn_branch = lax.psum_scatter(
-        contract(attended, wo_full), "tensor", scatter_dimension=0, tiled=True
-    )
-    hidden_res = residual + attn_branch
-    normed_two, factor_mlp = scaled_norm(hidden_res, mlp_gain)
-    normed_two_all = lax.all_gather(normed_two.astype(jnp.bfloat16), "tensor", axis=0, tiled=True)
-    wg_full, wu_full, wd_full = (
-        lax.all_gather(gate_weight, "dp", axis=0, tiled=True),
-        lax.all_gather(up_weight, "dp", axis=0, tiled=True),
-        lax.all_gather(down_weight, "dp", axis=0, tiled=True),
-    )
-    gate = jnp.dot(normed_two_all, wg_full, preferred_element_type=jnp.float32)
-    up_part = jnp.dot(normed_two_all, wu_full, preferred_element_type=jnp.float32)
-    sigmoid_gate = jax.nn.sigmoid(gate)
-    activated = gate * sigmoid_gate
-    inner = (activated * up_part).astype(jnp.bfloat16)
-    mlp_branch = lax.psum_scatter(
-        contract(inner, wd_full).astype(jnp.bfloat16), "tensor", scatter_dimension=0, tiled=True
-    ).astype(jnp.float32)
-    output = (hidden_res + mlp_branch).astype(jnp.bfloat16)
-    cotangent_all = lax.all_gather(cotangent, "tensor", axis=0, tiled=True)
-    wg_back, wu_back, wd_back = (
-        lax.all_gather(gate_weight, "dp", axis=0, tiled=True),
-        lax.all_gather(up_weight, "dp", axis=0, tiled=True),
-        lax.all_gather(down_weight, "dp", axis=0, tiled=True),
-    )
-    inner_grad = jnp.dot(cotangent_all, wd_back, preferred_element_type=jnp.float32)
-    gate_grad = (inner_grad * up_part * sigmoid_gate * (1.0 + gate * (1.0 - sigmoid_gate))).astype(
-        jnp.bfloat16
-    )
-    up_grad = (inner_grad * activated).astype(jnp.bfloat16)
-    down_wgrad = outer_sum(cotangent_all, inner)
-    gate_wgrad = outer_sum(normed_two_all, gate_grad)
-    up_wgrad = outer_sum(normed_two_all, up_grad)
-    normed_two_part = contract(gate_grad, wg_back) + contract(up_grad, wu_back)
-    normed_two_grad = lax.psum_scatter(
-        normed_two_part.astype(jnp.bfloat16), "tensor", scatter_dimension=0, tiled=True
-    ).astype(jnp.float32)
-    hidden_grad = cotangent.astype(jnp.float32) + norm_back(
-        hidden_res, factor_mlp, mlp_gain, normed_two_grad
-    )
-    mlp_gain_part = jnp.sum(normed_two_grad * hidden_res * factor_mlp, axis=0)
-    branch_all = lax.all_gather(hidden_grad.astype(jnp.bfloat16), "tensor", axis=0, tiled=True)
+    a_part = contract(attended, wo_full).astype(jnp.bfloat16)
+    groups = [[0, 1, 2, 3], [4, 5, 6, 7]]
+    cotangent_all = lax.all_gather(cotangent, "tensor", axis=0, tiled=True, axis_index_groups=groups)
+    w_all, n2_all, hidden_res = mlp_in(a_part, tokens, mlp_gain[None], gate_weight.T, up_weight.T, down_weight.T)
+    m_part, dn_part, grads = mlp(w_all, n2_all, cotangent_all)
+    output, hidden_grad, branch_all, mlp_gain_part, gate_wg, up_wg, down_wg = mlp_out(
+        m_part, dn_part, grads, hidden_res, mlp_gain[None], cotangent
+    )
+    mlp_gain_part = mlp_gain_part[0]
     wq_back, wk_back, wv_back, wo_back = (
         lax.all_gather(query_weight, "dp", axis=0, tiled=True),
         lax.all_gather(key_weight, "dp", axis=0, tiled=True),
@@ -277,15 +867,9 @@
         lax.psum_scatter(
             out_wgrad.astype(jnp.bfloat16), "dp", scatter_dimension=0, tiled=True
         ).astype(jnp.float32),
-        lax.psum_scatter(
-            gate_wgrad.astype(jnp.bfloat16), "dp", scatter_dimension=0, tiled=True
-        ).astype(jnp.float32),
-        lax.psum_scatter(
-            up_wgrad.astype(jnp.bfloat16), "dp", scatter_dimension=0, tiled=True
-        ).astype(jnp.float32),
-        lax.psum_scatter(
-            down_wgrad.astype(jnp.bfloat16), "dp", scatter_dimension=0, tiled=True
-        ).astype(jnp.float32),
+        gate_wg.T,
+        up_wg.T,
+        down_wg.T,
     )
     gain_sums = lax.psum((attn_gain_part, mlp_gain_part), ("dp", "tensor"))
     return (

time: 1420 us -> 945 us (0.67)
  waiting for transfers between devices: 1080 us -> 494 us
  Pallas kernels: 0 us -> 228 us
  matrix products: 128 us -> 68.8 us
  blocking collectives: 98.7 us -> 64.5 us
  local copies, waits for them, and re-layouts: 36 us -> 17.3 us
    all_gather x6 -> x1, waiting for transfers between devices: 253 us -> 0.02 us  [shards(): lax.all_gather(cotangent, 'tensor', axis=0, tiled=True, axis_index_groups...]
    pallas_call x0 -> x3, Pallas kernels: none -> 228 us  [the longest x1 86.7 us: mlp_out(): pl.pallas_call(mlp_out_kernel, name='mlp_out', out_shape=(jax.ShapeDtypeS...]
    unnamed x25 -> x11, waiting for transfers between devices: 159 us -> 3.04 us
    reduce_scatter x3 -> x0, waiting for transfers between devices: 143 us -> none  [the longest x1 90.6 us: shards(): lax.psum_scatter(contract(attended, wo_full), 'tensor', scatter_dimension...]
    psum x1, blocking collectives: 98.7 us -> 64.5 us  [shards(): gain_sums = lax.psum((attn_gain_part, mlp_gain_part), ('dp', 'tensor'))]
    reduce_scatter x1, waiting for transfers between devices: 68.2 us -> 36.7 us  [shards(): lax.psum_scatter(key_wgrad.astype(jnp.bfloat16), 'dp', scatter_dimension=...]
    dot_general x3 -> x0, matrix products: 25.5 us -> none  [the longest x1 10.1 us: shards(): jnp.dot(cotangent_all, wd_back, preferred_element_type=jnp.float32)]
    dot_general x7 -> x4, matrix products: 38.2 us -> 16.2 us  [outer_sum(): lax.dot_general(left, right, (((0,), (0,)), ((), ())), preferred_element_...]
  transfers between devices with their start and end apart: 22 -> 11, of which waited for: 21 -> 10; matrix products, arithmetic and copies ran while one was open for 12% -> 8% of each run, Pallas kernels for 0% -> 9%
where the time goes in v1:
time: 945 us; the launch traced here: 937 us
  waiting for transfers between devices  494 us (52%)
  Pallas kernels  228 us (24%)
  matrix products  68.8 us (7%)
  blocking collectives  64.5 us (7%)
  other arithmetic  40.3 us (4%)
  local copies, waits for them, and re-layouts  17.3 us (2%)
  between operations  14.8 us (2%)
    pallas_call x1, Pallas kernels, mlp_out(): pl.pallas_call(mlp_out_kernel, name='mlp_out', out_shape=(jax.ShapeDtypeS...  86.7 us
    pallas_call x1, Pallas kernels, mlp_in(): pl.pallas_call(mlp_in_kernel, name='mlp_in', out_shape=(jax.ShapeDtypeStr...  83.7 us
    reduce_scatter x1, waiting for transfers between devices, shards(): lax.psum_scatter(query_wgrad.astype(jnp.bfloat16), 'dp', scatter_dimensio...  69.2 us
    reduce_scatter x1, waiting for transfers between devices, shards(): lax.psum_scatter(value_wgrad.astype(jnp.bfloat16), 'dp', scatter_dimensio...  68.5 us
    reduce_scatter x1, waiting for transfers between devices, shards(): lax.psum_scatter(out_wgrad.astype(jnp.bfloat16), 'dp', scatter_dimension=...  68.1 us
    psum x1, blocking collectives, shards(): gain_sums = lax.psum((attn_gain_part, mlp_gain_part), ('dp', 'tensor'))  64.5 us
    pallas_call x1, Pallas kernels, mlp(): pl.pallas_call(mlp_kernel, name='mlp', out_shape=(jax.ShapeDtypeStruct((5...  57.6 us
    reduce_scatter x1, waiting for transfers between devices, shards(): lax.psum_scatter(normed_part.astype(jnp.bfloat16), 'tensor', scatter_dime...  55.2 us
  transfers between devices with their start and end apart: 11, of which 10 were waited for; matrix products, arithmetic and copies ran while one was open for 8% of the time, Pallas kernels for 9%

profile of v1, /device:TPU:1, one launch (start us, length us, event | category | flops | bytes accessed | tf_op | source)
XLA Modules:
  0.0 937.1 jit_solution(18413804581868069945)
XLA Ops:
  10.2 2.0 fusion.46
  16.5 1.9 multiply_cosine_fusion
  19.7 39.3 %all-gather.11.cloned.1.call-done = bf16[2048,256]{1,0:T(8,128)(2,1)} async-done(((bf16[128,256]{1,0:T(8,128)(2,1)}), bf16[2048,256]{1,0:T(8,128)(2,1)}) %all-gather.11.cloned.1.call-update) | async-done | bytes 1048592 | tf_op jit(solution)/shard_map/all_gather | solution.py:799
  58.9 53.4 %all-gather.7.cloned.1.call-done = bf16[1024,2048]{1,0:T(8,128)(2,1)} async-done(((bf16[128,2048]{1,0:T(8,128)(2,1)}), bf16[1024,2048]{1,0:T(8,128)(2,1)}) %all-gather.7.cloned.1.call-update) | async-done | bytes 4194320 | tf_op jit(solution)/shard_map/all_gather | solution.py:796
  112.3 3.8 fusion.63
  116.4 1.7 slice_negate_fusion.2
  118.1 40.5 %all-gather.9.cloned.1.call-done = bf16[2048,256]{1,0:T(8,128)(2,1)} async-done(((bf16[128,256]{1,0:T(8,128)(2,1)}), bf16[2048,256]{1,0:T(8,128)(2,1)}) %all-gather.9.cloned.1.call-update) | async-done | bytes 1048592 | tf_op jit(solution)/shard_map/all_gather | solution.py:798
  158.6 3.8 fusion.62
  162.7 1.7 slice_negate_fusion.3
  164.4 40.1 %all-gather.13.cloned.1.call-done = bf16[2048,256]{1,0:T(8,128)(2,1)} async-done(((bf16[128,256]{1,0:T(8,128)(2,1)}), bf16[2048,256]{1,0:T(8,128)(2,1)}) %all-gather.13.cloned.1.call-update) | async-done | bytes 1048592 | tf_op jit(solution)/shard_map/all_gather | solution.py:800
  204.5 3.8 convolution_convert_fusion.6
  208.6 3.4 fusion.56
  212.0 18.4 %while.27 = (s32[]{:T(128)}, bf16[2,512,2,128]{3,2,1,0:T(2,128)(2,1)}, f32[2,2,512]{2,1,0:T(2,128)S(1)}, s32[2]{0:T(128)S(1)}, s32[1024]{0:T(1024)S(1)}, /*index...) while((s32[]{:T(128)}, ...), condition=%wide.region_7.8_spmd, body=%wide.region_4.7_spmd.sunk | while | flops 551157248 | bytes 21018856 | solution.py:723
  218.7 1.7 fusion.120
  227.6 1.7 fusion.120
  230.4 19.9 %all-gather.15.cloned.1.call-done = bf16[2048,256]{1,0:T(8,128)(2,1)} async-done(((bf16[128,256]{1,0:T(8,128)(2,1)}), bf16[2048,256]{1,0:T(8,128)(2,1)}) %all-gather.15.cloned.1.call-update) | async-done | bytes 1048592 | tf_op jit(solution)/shard_map/all_gather | solution.py:801
  250.4 4.7 convolution_convert_fusion.a_part
  255.0 83.7 %mlp_in.1 = (bf16[3,2,688,2048]{3,2,1,0:T(8,128)(2,1)}, bf16[512,2048]{1,0:T(8,128)(2,1)}, f32[128,2048]{1,0:T(8,128)}) custom-call(bf16[1024,2048]{1,0:T(8,128)(2,1)} %convolution_convert_fusion.a_part, bf16[128,2048]{1,0:T(8,128)(2,1)} %tok.1, f32[1,2048]{1,0:T(1,128)} %bitcast.143, bf16[688,128]{1,0:T(8,128)(2,1)} %bitcast.140, ...), custom_call_target="tpu_custom_call" | custom-call | tf_op jit(solution)/shard_map/mlp_in/pallas_call | solution.py:415
  338.7 57.6 %mlp.1 = (bf16[512,2048]{1,0:T(8,128)(2,1)}, bf16[512,2048]{1,0:T(8,128)(2,1)}, bf16[3,2,688,2048]{3,2,1,0:T(8,128)(2,1)}) custom-call(bf16[3,2,688,2048]{3,2,1,0:T(8,128)(2,1)} %get-tuple-element.127.w_all, bf16[512,2048]{1,0:T(8,128)(2,1)} %get-tuple-element.128.n2_all, bf16[512,2048]{1,0:T(8,128)(2,1)} %all-gather.17.cloned.1.call-done.g_all), custom_call_target="tpu_custom_call" | custom-call | flops 25999998976 | bytes 41943040 | tf_op jit(solution)/shard_map/mlp/pallas_call | solution.py:508
  396.3 86.7 %mlp_out.1 = (bf16[128,2048]{1,0:T(8,128)(2,1)}, f32[128,2048]{1,0:T(8,128)}, bf16[1024,2048]{1,0:T(8,128)(2,1)}, f32[1,2048]{1,0:T(1,128)}, f32[688,128]{1,0:T(...) custom-call(bf16[512,2048]{1,0:T(8,128)(2,1)} %get-tuple-element.129.m_part, ...), custom_call_target="tpu_custom_call" | custom-call | tf_op jit(solution)/shard_map/mlp_out/pallas_call | solution.py:607
  483.0 3.5 convolution_convert_fusion.5
  486.5 32.7 %while.28 = (s32[]{:T(128)}, f32[1024,2,128]{0,2,1:T(8,128)}, f32[1024,2,128]{0,2,1:T(8,128)}, f32[2,512,2,128]{3,1,2,0:T(8,128)}, s32[2]{0:T(128)S(1)}, /*index...) while((s32[]{:T(128)}, f32[1024,2,128]{0,2,1:T(8,128)}, ...), condition=%wide.region_10.11_spmd.clone, body=%wide.region_8.10_spmd.clone.sunk | while | flops 1360920064 | bytes 87075776 | solution.py:767
  491.4 2.0 multiply_reduce_fusion.2
  494.8 2.7 fusion.132
  497.5 1.5 fusion.134
  499.0 3.6 fusion.133
  507.4 2.0 multiply_reduce_fusion.2
  510.8 3.0 fusion.132
  513.8 1.5 fusion.134
  515.3 3.9 fusion.133
  519.2 2.3 copy.83
  521.6 1.5 copy.85
  527.4 4.6 convolution_convert_fusion.3
  535.7 2.4 convolution_convert_fusion.4
  538.1 4.6 convolution_convert_fusion.1
  544.1 4.7 convolution_convert_fusion.2
  551.5 3.4 add_convert_fusion
  555.0 36.7 %reduce-scatter.10.cloned.1.call-done = bf16[128,256]{1,0:T(8,128)(2,1)} async-done(((bf16[2048,256]{1,0:T(8,128)(2,1)}), bf16[128,256]{1,0:T(8,128)(2,1)}) %reduce-scatter.10.cloned.1.call-update) | async-done | bytes 65552 | tf_op jit(solution)/shard_map/reduce_scatter | solution.py:861
  591.7 1.5 convert_element_type.103
  593.2 69.2 %reduce-scatter.8.cloned.1.call-done = bf16[128,256]{1,0:T(8,128)(2,1)} async-done(((bf16[2048,256]{1,0:T(8,128)(2,1)}), bf16[128,256]{1,0:T(8,128)(2,1)}) %reduce-scatter.8.cloned.1.call-update) | async-done | bytes 65552 | tf_op jit(solution)/shard_map/reduce_scatter | solution.py:858
  662.4 1.5 convert_element_type.101
  663.9 68.1 %reduce-scatter.14.cloned.1.call-done = bf16[128,256]{1,0:T(8,128)(2,1)} async-done(((bf16[2048,256]{1,0:T(8,128)(2,1)}), bf16[128,256]{1,0:T(8,128)(2,1)}) %reduce-scatter.14.cloned.1.call-update) | async-done | bytes 65552 | tf_op jit(solution)/shard_map/reduce_scatter | solution.py:867
  732.0 1.5 convert_element_type.107
  733.5 68.5 %reduce-scatter.12.cloned.1.call-done = bf16[128,256]{1,0:T(8,128)(2,1)} async-done(((bf16[2048,256]{1,0:T(8,128)(2,1)}), bf16[128,256]{1,0:T(8,128)(2,1)}) %reduce-scatter.12.cloned.1.call-update) | async-done | bytes 65552 | tf_op jit(solution)/shard_map/reduce_scatter | solution.py:864
  802.0 1.5 convert_element_type.105
  803.5 55.2 %reduce-scatter.6.cloned.1.call-done = bf16[128,2048]{1,0:T(8,128)(2,1)} async-done(((bf16[1024,2048]{1,0:T(8,128)(2,1)}), bf16[128,2048]{1,0:T(8,128)(2,1)}) %reduce-scatter.6.cloned.1.call-update) | async-done | bytes 524304 | tf_op jit(solution)/shard_map/reduce_scatter | solution.py:852
  860.1 64.5 %all-reduce = (f32[2048]{0:T(1024)}, f32[2048]{0:T(1024)}) all-reduce(f32[2048]{0:T(1024)S(1)} %get-tuple-element.256, f32[2048]{0:T(1024)S(1)} %bitcast.145), channel_id=1, replica_groups=mesh['dp'=16,'tensor'=8] {'dp','tensor'}, use_global_device_ids=true, to_apply=%region_14.15 | all-reduce | flops 4096 | bytes 32768 | tf_op jit(solution)/shard_map/psum | solution.py:874
  924.6 2.5 fusion.43
  (168 shorter events, 44.6 us)
Async XLA Ops:
  7.2 51.7 %all-gather.11.cloned.1.call-start = ((), (), s32[]{:S(2)}) async-start(), calls=%async_computation.7 | async-start | bytes 1114112 | tf_op jit(solution)/shard_map/all_gather | solution.py:799
  7.9 104.4 %all-gather.7.cloned.1.call-start = ((), (), s32[]{:S(2)}) async-start(), calls=%async_computation.5 | async-start | bytes 4718592 | tf_op jit(solution)/shard_map/all_gather | solution.py:796
  12.3 146.3 %all-gather.9.cloned.1.call-start = ((), (), s32[]{:S(2)}) async-start(), calls=%async_computation.6 | async-start | bytes 1114112 | tf_op jit(solution)/shard_map/all_gather | solution.py:798
  13.0 191.5 %all-gather.13.cloned.1.call-start = ((), (), s32[]{:S(2)}) async-start(), calls=%async_computation.8 | async-start | bytes 1114112 | tf_op jit(solution)/shard_map/all_gather | solution.py:800
  13.6 236.8 %all-gather.15.cloned.1.call-start = ((), (), s32[]{:S(2)}) async-start(), calls=%async_computation.9 | async-start | bytes 1114112 | tf_op jit(solution)/shard_map/all_gather | solution.py:801
  14.2 324.5 %all-gather.17.cloned.1.call-start = ((), (), s32[]{:S(2)}) async-start(), calls=%async_computation.10 | async-start | bytes 2621440 | tf_op jit(solution)/shard_map/all_gather | solution.py:817
  14.8 576.9 %reduce-scatter.10.cloned.1.call-start = ((), (), s32[]{:S(2)}) async-start(), calls=%async_computation.13 | async-start | bytes 1114112 | tf_op jit(solution)/shard_map/reduce_scatter | solution.py:861
  162.7 45.8 %copy-start.6 = (f32[1024,2,128]{2,0,1:T(8,128)}, f32[1024,2,128]{2,0,1:T(8,128)S(1)}, u32[]{:S(2)}) copy-start(f32[1024,2,128]{2,0,1:T(8,128)S(1)} %copy.71) | copy-start | bytes 3145732
  218.7 1.7 copy-start.13
  227.6 1.7 copy-start.13
  396.3 86.7 %copy-start.19 = (bf16[2048,256]{1,0:T(8,128)(2,1)S(1)}, bf16[2048,256]{1,0:T(8,128)(2,1)}, u32[]{:S(2)}) copy-start(bf16[2048,256]{1,0:T(8,128)(2,1)} %all-gather.15.cloned.1.call-done) | copy-start | bytes 3145732
  486.7 6.7 copy-start.2
  486.7 6.7 copy-start.4
  486.7 6.7 copy-start.11
  491.4 2.0 copy-start
  494.8 4.2 copy-start.1
  499.0 3.6 copy-start.3
  499.0 3.6 copy-start.5
  499.0 3.6 copy-start.12
  502.6 6.7 copy-start.2
  502.6 6.7 copy-start.4
  502.6 6.7 copy-start.11
  507.3 2.0 copy-start
  510.7 4.5 copy-start.1
  515.3 3.9 copy-start.3
  515.3 3.9 copy-start.5
  515.3 3.9 copy-start.12
  519.2 3.9 copy-start.9
  523.1 1.8 copy-start.8
  527.3 4.9 copy-start.10
  532.0 130.4 %reduce-scatter.8.cloned.1.call-start = ((), (), s32[]{:S(2)}) async-start(), calls=%async_computation.12 | async-start | bytes 1114112 | tf_op jit(solution)/shard_map/reduce_scatter | solution.py:858
  533.5 2.2 copy-start.30
  535.7 2.4 copy-start.15
  538.1 193.9 %reduce-scatter.14.cloned.1.call-start = ((), (), s32[]{:S(2)}) async-start(), calls=%async_computation.15 | async-start | bytes 1114112 | tf_op jit(solution)/shard_map/reduce_scatter | solution.py:867
  542.8 259.2 %reduce-scatter.12.cloned.1.call-start = ((), (), s32[]{:S(2)}) async-start(), calls=%async_computation.14 | async-start | bytes 1114112 | tf_op jit(solution)/shard_map/reduce_scatter | solution.py:864
  544.1 4.7 copy-start.16
  548.8 309.9 %reduce-scatter.6.cloned.1.call-start = ((), (), s32[]{:S(2)}) async-start(), calls=%async_computation.11 | async-start | bytes 4718592 | tf_op jit(solution)/shard_map/reduce_scatter | solution.py:852
  548.9 1.3 copy-start.17
  554.9 303.8 %copy-start.7 = (bf16[128,2048]{1,0:T(8,128)(2,1)S(1)}, bf16[128,2048]{1,0:T(8,128)(2,1)}, u32[]{:S(2)}) copy-start(bf16[128,2048]{1,0:T(8,128)(2,1)} %tok.1) | copy-start | bytes 1572868
  554.9 303.8 %copy-start.25 = (f32[2048]{0:T(1024)S(1)}, f32[2048]{0:T(1024)}, u32[]{:S(2)}) copy-start(f32[2048]{0:T(1024)} %param.18) | copy-start | bytes 24580
  554.9 303.8 %copy-start.28 = (f32[128]{0:T(128)S(1)}, f32[128]{0:T(128)}, u32[]{:S(2)}) copy-start(f32[128]{0:T(128)} %copy-done.27) | copy-start | bytes 1540
  554.9 305.2 %copy-start.26 = (f32[1,2048]{1,0:T(1,128)S(1)}, f32[1,2048]{1,0:T(1,128)}, u32[]{:S(2)}) copy-start(f32[1,2048]{1,0:T(1,128)} %get-tuple-element.140) | copy-start | bytes 24580
  554.9 369.7 %copy-start.20 = (f32[128,2048]{1,0:T(8,128)S(1)}, f32[128,2048]{1,0:T(8,128)}, u32[]{:S(2)}) copy-start(f32[128,2048]{1,0:T(8,128)} %get-tuple-element.134) | copy-start | bytes 3145732
  554.9 369.7 %copy-start.29 = (f32[128]{0:T(128)S(1)}, f32[128]{0:T(128)}, u32[]{:S(2)}) copy-start(f32[128]{0:T(128)} %get-tuple-element.318) | copy-start | bytes 1540
  554.9 372.2 %copy-start.21 = (bf16[128,2048]{1,0:T(8,128)(2,1)S(1)}, bf16[128,2048]{1,0:T(8,128)(2,1)}, u32[]{:S(2)}) copy-start(bf16[128,2048]{1,0:T(8,128)(2,1)} %get-tuple-element.532) | copy-start | bytes 1572868
  554.9 372.9 %copy-start.24 = (f32[688,128]{1,0:T(8,128)S(1)}, f32[688,128]{1,0:T(8,128)}, u32[]{:S(2)}) copy-start(f32[688,128]{1,0:T(8,128)} %get-tuple-element.141) | copy-start | bytes 1056772
  555.0 373.6 %copy-start.23 = (f32[688,128]{1,0:T(8,128)S(1)}, f32[688,128]{1,0:T(8,128)}, u32[]{:S(2)}) copy-start(f32[688,128]{1,0:T(8,128)} %get-tuple-element.142) | copy-start | bytes 1056772
  555.0 374.4 %copy-start.22 = (f32[688,128]{1,0:T(8,128)S(1)}, f32[688,128]{1,0:T(8,128)}, u32[]{:S(2)}) copy-start(f32[688,128]{1,0:T(8,128)} %get-tuple-element.143) | copy-start | bytes 1056772
  (4 other events, 3.4 us)
Sparse Core Ops, SparseCore 0:
  10.5 48.3 all-gather.10
  61.1 51.1 all-gather.6
  114.8 43.8 all-gather.8
  160.9 43.5 all-gather.12
  206.8 43.5 all-gather.14
  251.9 46.3 all-gather.16
  532.1 59.5 reduce-scatter.9
  596.5 65.8 reduce-scatter.7
  666.1 65.8 reduce-scatter.13
  736.1 65.8 reduce-scatter.11
  804.4 54.2 reduce-scatter.5

commit v2 on v1

--- a/solution.py
+++ b/solution.py
@@ -2,13 +2,13 @@
 
 import jax
 import jax.numpy as jnp
+import numpy as np
 from jax import lax
 from jax.experimental import pallas as pl
 from jax.experimental.pallas import tpu as pltpu
 from jax.sharding import PartitionSpec as P
 
 HEAD_DIM = 128
-QBLOCK = 512
 EPS = 1e-05
 THETA = 10000.0
 D = 2048
@@ -19,6 +19,8 @@
 MESH = pl.DeviceIdType.MESH
 ANY = pl.BlockSpec(memory_space=pl.ANY)
 VMEM = pl.BlockSpec(memory_space=pltpu.VMEM)
+NT = (((1,), (1,)), ((), ()))
+TN = (((0,), (0,)), ((), ()))
 
 
 class Net:
@@ -181,14 +183,22 @@
                + got[4 + k, pl.ds(pl.multiple_of(at - 64 * k, 16), 16), :].astype(jnp.float32))
 
 
-def reduce_8(net, part, sums, got, sums_half, got_half, out):
+def reduce_8(net, make, part, sums, got, sums_half, got_half, out):
     up, down, beside = net.device(dz=1), net.device(dz=-1), net.beside
     xl, z = net.xl, net.z
+    make(1 - xl, z + 2)
     a = net.send(part.at[block8(1 - xl, z + 2), :], got.at[0], beside)
+    make(1 - xl, z + 1)
     b0 = net.send(part.at[block8(1 - xl, z + 1), :], got.at[1], up)
+    make(1 - xl, z - 1)
     b1 = net.send(part.at[block8(1 - xl, z - 1), :], got.at[2], down)
+    make(xl, z + 2)
+    make(xl, z + 1)
     d1 = net.send(part.at[half8(xl, z + 1, 1), :], got_half.at[3], up)
+    make(xl, z - 1)
     d2 = net.send(part.at[half8(xl, z - 1, 0), :], got_half.at[4], down)
+    make(1 - xl, z)
+    make(xl, z)
     yield
     a.wait_recv()
     add_rows(128, sums.at[0], part.at[block8(xl, z + 2), :], got.at[0])
@@ -375,7 +385,7 @@
     return ref.at[:, lax.rem(x, 2), :, at]
 
 
-def mlp_in_kernel(a_part, tok, gain, wg, wu, wd, w_all, n2_all, h1, n2, sums, got, sums_half, got_half, send_sems, recv_sems, sems):
+def mlp_in_kernel(o, wo, tok, gain, wg, wu, wd, w_all, n2_all, h1, a_part, n2, sums, got, sums_half, got_half, send_sems, recv_sems, sems):
     net = Net(send_sems, recv_sems)
     xy = [net.device(dx=1), net.device(dx=-1), net.device(dy=1), net.device(dy=-1)]
     own = ff_slab(net, w_all, net.c, 0, 0)
@@ -386,7 +396,12 @@
 
     def tokens():
         out = []
-        yield from reduce_8(net, a_part, sums, got, sums_half, got_half, out)
+
+        def make(xl, z):
+            here = block8(xl, z)
+            a_part[here, :] = lax.dot_general(o[here, :], wo[...], NT, preferred_element_type=jnp.float32).astype(jnp.bfloat16)
+
+        yield from reduce_8(net, make, a_part, sums, got, sums_half, got_half, out)
 
         def step(at, k):
             here = pl.ds(at, 16)
@@ -411,7 +426,7 @@
     net.finish()
 
 
-def mlp_in(a_part, tok, gain, wg, wu, wd):
+def mlp_in(o, wo, tok, gain, wg, wu, wd):
     return pl.pallas_call(
         mlp_in_kernel,
         name="mlp_in",
@@ -420,9 +435,10 @@
             jax.ShapeDtypeStruct((4 * ROWS, D), jnp.bfloat16),
             jax.ShapeDtypeStruct((ROWS, D), jnp.float32),
         ),
-        in_specs=[VMEM, VMEM, VMEM, ANY, ANY, ANY],
+        in_specs=[VMEM, VMEM, VMEM, VMEM, ANY, ANY, ANY],
         out_specs=(ANY, ANY, VMEM),
         scratch_shapes=[
+            pltpu.VMEM((GROUP, D), jnp.bfloat16),
             pltpu.VMEM((ROWS, D), jnp.bfloat16),
             pltpu.VMEM((2, ROWS, D), jnp.bfloat16),
             pltpu.VMEM((4, ROWS, D), jnp.bfloat16),
@@ -433,10 +449,9 @@
             pltpu.SemaphoreType.DMA((4,)),
         ],
         compiler_params=pltpu.CompilerParams(collective_id=1, has_side_effects=True, vmem_limit_bytes=56 << 20),
-    )(a_part, tok, gain, wg, wu, wd)
-
-
-NT = (((1,), (1,)), ((), ()))
+    )(o, wo, tok, gain, wg, wu, wd)
+
+
 TILES = ((0, 256), (256, 256), (512, 176))
 
 
@@ -635,139 +650,335 @@
     )(m_part, dn_part, grads, h1, gain, cot)
 
 
-def places(lengths_row, group_rows):
-    seq_ends = jnp.cumsum(lengths_row)
-    indices = jnp.arange(group_rows, dtype=jnp.int32)
-    passed = indices[:, None] >= seq_ends[None, :]
-    segment = jnp.sum(passed.astype(jnp.int32), axis=1)
-    seq_start = jnp.sum(jnp.where(passed, lengths_row[None, :], 0), axis=1)
-    return (segment, indices - seq_start)
-
-
-def rotary(position, head_width):
-    half_width = head_width // 2
-    rates = THETA ** (-(jnp.arange(half_width, dtype=jnp.float32) * 2.0 / head_width))
-    angles = position.astype(jnp.float32)[:, None] * rates[None, :]
-    rot_cos = jnp.cos(angles)
-    rot_sin = jnp.sin(angles)
-    return (jnp.concatenate([rot_cos, rot_cos], 1), jnp.concatenate([rot_sin, rot_sin], 1))
-
-
-def rotate(vector, rot_cos, rot_sin):
-    half_width = vector.shape[-1] // 2
-    turned = jnp.concatenate([-vector[..., half_width:], vector[..., :half_width]], -1)
-    return vector * rot_cos[:, None, :] + turned * rot_sin[:, None, :]
-
-
-def rotate_back(grad_rows, rot_cos, rot_sin):
-    half_width = grad_rows.shape[-1] // 2
-    moved = grad_rows * rot_sin[:, None, :]
-    turned = jnp.concatenate([-moved[..., half_width:], moved[..., :half_width]], -1)
-    return grad_rows * rot_cos[:, None, :] - turned
-
-
-def scaled_norm(vector, gain_row):
-    factor = lax.rsqrt(jnp.mean(vector * vector, axis=-1, keepdims=True) + EPS)
-    return (vector * factor * gain_row, factor)
-
-
-def norm_back(vector, factor, gain_row, grad_rows):
-    inner = grad_rows * gain_row
-    return factor * inner - vector * (factor * factor * factor) * jnp.mean(
-        vector * inner, axis=-1, keepdims=True
+ATT_CUT = (lambda ref: ref.at[:, pl.ds(0, 64), :], lambda ref: ref.at[:, pl.ds(64, 64), :])
+ATT_CUT_T = (lambda ref: ref.at[:, pl.ds(0, 128), :], lambda ref: ref.at[:, pl.ds(128, 128), :])
+
+
+def att_at(net, kind, i, j):
+    x, y = lax.rem(net.x + 2 * i + 4, 4), lax.rem(net.y + j + 4, 4)
+    return pl.ds(pl.multiple_of((y * 4 + lax.div(x, 2) * 2 + kind) * 128, 128), 128)
+
+
+def sequence_starts(lengths, at, rows):
+    index = lax.broadcasted_iota(jnp.int32, (rows, 1), 0) + at
+    end, start = lengths[0, 0], jnp.zeros((rows, 1), jnp.int32)
+    for s in range(8):
+        start = jnp.where(index >= end, end, start)
+        if s < 7:
+            end = end + lengths[0, s + 1]
+    return index, start
+
+
+QROWS = 256
+
+
+def attn_in_kernel(tok, cot, lengths, gain, rates, wq, wk, wv, wo,
+                   g_all, n1_out, w_out, q_out, k_out, v_out, p_out, o_out, table_out,
+                   n1, n1_all, w, q, k, v, p, o, table, send_sems, recv_sems, sems):
+    net = Net(send_sems, recv_sems)
+    own_rows = att_at(net, net.c, 0, 0)
+    copies = [pltpu.make_async_copy(u, w.at[m, own_rows, :], sems.at[m]) for m, u in enumerate((wq, wk, wv, wo))]
+    for copy in copies:
+        copy.start()
+    copies.append(pltpu.make_async_copy(cot, g_all.at[block(net.z), :], sems.at[4]))
+    copies[4].start()
+
+    def norm(at, _):
+        here = pl.ds(at, 16)
+        value = tok[here, :].astype(jnp.float32)
+        r = lax.rsqrt(jnp.mean(value * value, axis=-1, keepdims=True) + EPS)
+        n1[here, :] = (value * r * gain[...]).astype(jnp.bfloat16)
+
+    each_half(norm)
+    net.greet([net.device(dy=1), net.device(dy=-1), net.device(dz=1), net.device(dz=-1), net.device(dc=1), net.beside, net.across])
+    place = pltpu.make_async_copy(n1, n1_all.at[block8(net.xl, net.z), :], sems.at[5])
+    place.start()
+
+    def tokens():
+        yield from gather_8(net, n1, n1_all)
+
+    def cotangent():
+        yield from gather_z(net, cot, g_all)
+
+    def weights():
+        for copy in copies[:4]:
+            copy.wait()
+
+        def slab(i, j):
+            return w.at[:, att_at(net, net.c, i, j), :]
+
+        yield from gather_plane(net, slab, ATT_CUT, (net.across,), (net.device(dy=1), net.device(dy=-1)))
+
+    chains = {"t": tokens(), "w": weights(), "g": cotangent()}
+    for name in "tw":
+        next(chains[name])
+
+    def tables(i, _):
+        at = pl.multiple_of(i * 128, 128)
+        index, start = sequence_starts(lengths, at, 128)
+        angle = (index - start).astype(jnp.float32) * rates[...]
+        lane = lax.broadcasted_iota(jnp.int32, (128, 128), 1)
+        table[0, pl.ds(at, 128), :] = jnp.cos(angle)
+        sin = jnp.sin(angle)
+        table[1, pl.ds(at, 128), :] = jnp.where(lane < 64, -sin, sin)
+        return 0
+
+    lax.fori_loop(0, 8, tables, 0)
+    for name in "wttwt":
+        next(chains[name], None)
+    for name in "tw":
+        for _ in chains[name]:
+            pass
+    place.wait()
+    next(chains["g"])
+    saves = [
+        pltpu.make_async_copy(n1_all, n1_out, sems.at[6]),
+        pltpu.make_async_copy(w, w_out, sems.at[7]),
+        pltpu.make_async_copy(table, table_out, sems.at[8]),
+    ]
+    for copy in saves:
+        copy.start()
+
+    def project(i, _):
+        here = pl.ds(pl.multiple_of(i * QROWS, QROWS), QROWS)
+        left = n1_all[here, :]
+        cos, sin = table[0, here, :], table[1, here, :]
+        for m, dst in ((0, q), (1, k)):
+            u = jnp.dot(left, w[m], preferred_element_type=jnp.float32)
+            for h in range(2):
+                uh = u[:, h * 128 : h * 128 + 128]
+                dst[h, here, :] = (uh * cos + pltpu.roll(uh, 64, 1) * sin).astype(jnp.bfloat16)
+        u = jnp.dot(left, w[2], preferred_element_type=jnp.float32).astype(jnp.bfloat16)
+        for h in range(2):
+            v[h, here, :] = u[:, h * 128 : h * 128 + 128]
+        return 0
+
+    lax.fori_loop(0, GROUP // QROWS, project, 0)
+    next(chains["g"], None)
+
+    for b in range(GROUP // QROWS):
+        rows = slice(b * QROWS, b * QROWS + QROWS)
+        first, last = max(0, b - 2) * QROWS, (b + 1) * QROWS
+        index, start = sequence_starts(lengths, b * QROWS, QROWS)
+        key = lax.broadcasted_iota(jnp.int32, (QROWS, last - first), 1) + first
+        allowed = (key <= index) & (key >= start)
+
+        for h in range(2):
+            s = lax.dot_general(q[h, rows, :], k[h, first:last, :], NT, preferred_element_type=jnp.float32)
+            s = jnp.where(allowed, s * HEAD_DIM ** (-0.5), -1e30)
+            e = jnp.exp(s - jnp.max(s, axis=-1, keepdims=True))
+            weights_b = (e / jnp.sum(e, axis=-1, keepdims=True)).astype(jnp.bfloat16)
+            p[h, rows, first:last] = weights_b
+            o[rows, h * 128 : h * 128 + 128] = jnp.dot(
+                weights_b, v[h, first:last, :], preferred_element_type=jnp.float32
+            ).astype(jnp.bfloat16)
+
+    more = [pltpu.make_async_copy(src, dst, sems.at[9 + n]) for n, (src, dst) in enumerate(((q, q_out), (k, k_out), (v, v_out), (p, p_out), (o, o_out)))]
+    for copy in more:
+        copy.start()
+    for _ in chains["g"]:
+        pass
+    for copy in copies[4:] + saves + more:
+        copy.wait()
+    net.finish()
+
+
+def attn_in(tok, cot, lengths, gain, rates, wq, wk, wv, wo):
+    bf, f32 = jnp.bfloat16, jnp.float32
+    shapes = (
+        ((4 * ROWS, D), bf), ((GROUP, D), bf), ((4, D, 256), bf), ((2, GROUP, 128), bf), ((2, GROUP, 128), bf),
+        ((2, GROUP, 128), bf), ((2, GROUP, GROUP), bf), ((GROUP, 256), bf), ((2, GROUP, 128), f32),
     )
-
-
-def contract(left, right):
-    return lax.dot_general(
-        left, right, (((1,), (1,)), ((), ())), preferred_element_type=jnp.float32
-    )
-
-
-def outer_sum(left, right):
-    return lax.dot_general(
-        left, right, (((0,), (0,)), ((), ())), preferred_element_type=jnp.float32
-    )
-
-
-def allowed_mask(segment, offset, block):
-    group_rows = segment.shape[0]
-    indices = jnp.arange(group_rows, dtype=jnp.int32)
-    query_at = offset + jnp.arange(block, dtype=jnp.int32)
-    seg_block = lax.dynamic_slice_in_dim(segment, offset, block, 0)
-    return (seg_block[:, None] == segment[None, :]) & (indices[None, :] <= query_at[:, None])
-
-
-def attention_forward(queries, key_rows, value_rows, segment, block):
-    group_rows, head_count, head_width = queries.shape
-    score_scale = head_width ** (-0.5)
-
-    def one_block(offset):
-        query_block = lax.dynamic_slice_in_dim(queries, offset, block, 0)
-        allowed = allowed_mask(segment, offset, block)
-        scores = (
-            jnp.einsum("qhd,khd->hqk", query_block, key_rows, preferred_element_type=jnp.float32)
-            * score_scale
+    return pl.pallas_call(
+        attn_in_kernel,
+        name="attn_in",
+        out_shape=tuple(jax.ShapeDtypeStruct(*s) for s in shapes),
+        in_specs=[VMEM, VMEM, pl.BlockSpec(memory_space=pltpu.SMEM), VMEM, VMEM, ANY, ANY, ANY, ANY],
+        out_specs=(ANY,) * 9,
+        scratch_shapes=[pltpu.VMEM((ROWS, D), bf)] + [pltpu.VMEM(*s) for s in shapes[1:]] + [
+            pltpu.SemaphoreType.DMA((48,)),
+            pltpu.SemaphoreType.DMA((48,)),
+            pltpu.SemaphoreType.DMA((14,)),
+        ],
+        compiler_params=pltpu.CompilerParams(collective_id=3, has_side_effects=True, vmem_limit_bytes=56 << 20),
+    )(tok, cot, lengths, gain, rates, wq, wk, wv, wo)
+
+
+def add_att(part, dst, *terms):
+    def step(m, _):
+        for at in {None: (0, 128), 0: (0,), 1: (128,)}[part]:
+            total = dst[m, at : at + 128, :].astype(jnp.float32)
+            for term in terms:
+                total = total + term[m, at : at + 128, :].astype(jnp.float32)
+            dst[m, at : at + 128, :] = total.astype(dst.dtype)
+        return 0
+
+    lax.fori_loop(0, 4, step, 0)
+
+
+def attn_out_kernel(da_in, n1_in, w_in, q_in, k_in, v_in, p_in, o_in, table_in, tok, dh1, gain, mlp_gain_part,
+                    dx, gains, gq, gk, gv, go,
+                    da, n1, w, q, k, v, p, o, table, do, dqkv, dk, dv, part, sums, got, sums_half, got_half,
+                    ga, sib, slab_half, slab_up, slab_down, slab_last, sum_z, sum_x, sum_y, sum_c,
+                    send_sems, recv_sems, sems):
+    net = Net(send_sems, recv_sems)
+    bf, f32 = jnp.bfloat16, jnp.float32
+    loads = [
+        pltpu.make_async_copy(src, dst, sems.at[m])
+        for m, (src, dst) in enumerate(((da_in, da), (w_in, w), (v_in, v), (p_in, p), (q_in, q), (k_in, k), (o_in, o), (table_in, table), (n1_in, n1)))
+    ]
+    for copy in loads:
+        copy.start()
+    line_x = [net.device(dx=s) for s in (1, 2, 3)]
+    line_y = [net.device(dy=s) for s in (1, 2, 3)]
+    line_z = [net.device(dz=s) for s in (1, 2, 3)]
+    net.greet(line_x + line_y + line_z + [net.device(dc=1)])
+    for copy in loads[:2]:
+        copy.wait()
+
+    def back(i, _):
+        here = pl.ds(pl.multiple_of(i * QROWS, QROWS), QROWS)
+        u = jnp.dot(da[here, :], w[3], preferred_element_type=f32).astype(bf)
+        for h in range(2):
+            do[h, here, :] = u[:, h * 128 : h * 128 + 128]
+        return 0
+
+    lax.fori_loop(0, GROUP // QROWS, back, 0)
+    for copy in loads[2:]:
+        copy.wait()
+    for h in range(2):
+        for b in range(GROUP // QROWS):
+            rows = slice(b * QROWS, b * QROWS + QROWS)
+            first, last = max(0, b - 2) * QROWS, (b + 1) * QROWS
+            keys = slice(first, last)
+            old = slice(first, b * QROWS)
+            weights_b = p[h, rows, keys]
+            do_b = do[h, rows, :]
+            dp = lax.dot_general(do_b, v[h, keys, :], NT, preferred_element_type=f32)
+            wide = weights_b.astype(f32)
+            centre = jnp.sum(wide * dp, axis=-1, keepdims=True)
+            ds = (wide * (dp - centre)).astype(bf)
+            dvb = lax.dot_general(weights_b, do_b, TN, preferred_element_type=f32)
+            dkb = lax.dot_general(ds, q[h, rows, :], TN, preferred_element_type=f32)
+            if b > 0:
+                dv[h, old, :] += dvb[: b * QROWS - first]
+                dk[h, old, :] += dkb[: b * QROWS - first]
+            dv[h, rows, :] = dvb[b * QROWS - first :]
+            dk[h, rows, :] = dkb[b * QROWS - first :]
+            dqb = jnp.dot(ds, k[h, keys, :], preferred_element_type=f32) * HEAD_DIM ** (-0.5)
+            dqb = dqb * table[0, rows, :] - pltpu.roll(dqb, 64, 1) * table[1, rows, :]
+            dqkv[rows, h * 128 : h * 128 + 128] = dqb.astype(bf)
+
+    def turn(i, _):
+        here = pl.ds(pl.multiple_of(i * QROWS, QROWS), QROWS)
+        for h in range(2):
+            u = dk[h, here, :] * HEAD_DIM ** (-0.5)
+            u = u * table[0, here, :] - pltpu.roll(u, 64, 1) * table[1, here, :]
+            dqkv[here, 256 + h * 128 : 384 + h * 128] = u.astype(bf)
+            dqkv[here, 512 + h * 128 : 640 + h * 128] = dv[h, here, :].astype(bf)
+        return 0
+
+    lax.fori_loop(0, GROUP // QROWS, turn, 0)
+    sum_z[net.z, 0:1, :] = jnp.zeros((1, D), f32)
+    sum_z[net.z, 1:2, :] = mlp_gain_part[...]
+
+    def make(xl, z):
+        here = block8(xl, z)
+        left = dqkv[here, :]
+
+        def columns(i, _):
+            at = pl.ds(pl.multiple_of(i * 512, 512), 512)
+            u = lax.dot_general(left[:, :256], w[0, at, :], NT, preferred_element_type=f32)
+            u = u + lax.dot_general(left[:, 256:512], w[1, at, :], NT, preferred_element_type=f32)
+            u = u + lax.dot_general(left[:, 512:], w[2, at, :], NT, preferred_element_type=f32)
+            part[here, at] = u.astype(bf)
+            sum_z[net.z, 0:1, at] += jnp.sum(u * n1[here, at].astype(f32), axis=0, keepdims=True)
+            return 0
+
+        lax.fori_loop(0, 4, columns, 0)
+
+    def tokens():
+        out = []
+        yield from reduce_8(net, make, part, sums, got, sums_half, got_half, out)
+
+        def step(at, k):
+            here = pl.ds(at, 16)
+            value = tok[here, :].astype(f32)
+            r = lax.rsqrt(jnp.mean(value * value, axis=-1, keepdims=True) + EPS)
+            inner = out[0](at, k) * gain[...]
+            dx[here, :] = dh1[here, :] + r * inner - value * (r * r * r) * jnp.mean(value * inner, axis=-1, keepdims=True)
+
+        each_half(step)
+
+    def weights():
+        def outer(i, _):
+            at = pl.ds(pl.multiple_of(i * 256, 256), 256)
+            u = lax.dot_general(dqkv[...], n1[:, at], TN, preferred_element_type=f32)
+            for m in range(3):
+                ga[m, :, at] = u[m * 256 : m * 256 + 256].astype(bf)
+            ga[3, :, at] = lax.dot_general(o[...], da[:, at], TN, preferred_element_type=f32).astype(bf)
+            return 0
+
+        lax.fori_loop(0, 8, outer, 0)
+
+        def slab(kind):
+            return lambda i, j: ga.at[:, :, att_at(net, kind, i, j)]
+
+        yield from reduce_plane(
+            net, slab(net.c), slab(1 - net.c), lambda i, j: sib.at[i, j], lambda i: slab_half.at[i], lambda i: slab_up.at[i],
+            lambda i: slab_down.at[i], lambda i: slab_last.at[i], ATT_CUT_T, add_att, (net.across,), (net.device(dy=1), net.device(dy=-1)),
         )
-        scores = jnp.where(allowed[None], scores, -1e30)
-        row_max = jnp.max(scores, axis=-1, keepdims=True)
-        raised = jnp.exp(scores - row_max)
-        totals = jnp.sum(raised, axis=-1, keepdims=True)
-        weights = (raised / totals).astype(jnp.bfloat16)
-        mixed_out = jnp.einsum(
-            "hqk,khd->qhd", weights, value_rows, preferred_element_type=jnp.float32
-        )
-        return (mixed_out.astype(jnp.bfloat16), (row_max + jnp.log(totals))[..., 0])
-
-    offsets = jnp.arange(group_rows // block, dtype=jnp.int32) * block
-    mixed_out, log_totals = lax.map(one_block, offsets)
-    return (mixed_out.reshape(group_rows, head_count * head_width), log_totals)
-
-
-def attention_backward(queries, key_rows, value_rows, segment, log_totals, out_grad, block):
-    group_rows, head_count, head_width = queries.shape
-    score_scale = head_width ** (-0.5)
-
-    def back_step(carried, block_in):
-        key_grad, value_grad = carried
-        offset, lse_block = block_in
-        query_block = lax.dynamic_slice_in_dim(queries, offset, block, 0)
-        grad_block = lax.dynamic_slice_in_dim(out_grad, offset, block, 0)
-        allowed = allowed_mask(segment, offset, block)
-        scores = (
-            jnp.einsum("qhd,khd->hqk", query_block, key_rows, preferred_element_type=jnp.float32)
-            * score_scale
-        )
-        scores = jnp.where(allowed[None], scores, -1e30)
-        probs = jnp.exp(scores - lse_block[..., None])
-        weights = probs.astype(jnp.bfloat16)
-        value_grad = value_grad + jnp.einsum(
-            "hqk,qhd->khd", weights, grad_block, preferred_element_type=jnp.float32
-        )
-        prob_grad = jnp.einsum(
-            "qhd,khd->hqk", grad_block, value_rows, preferred_element_type=jnp.float32
-        )
-        centre = jnp.sum(probs * prob_grad, axis=-1, keepdims=True)
-        score_grad = (probs * (prob_grad - centre)).astype(jnp.bfloat16)
-        query_grad = (
-            jnp.einsum("hqk,khd->qhd", score_grad, key_rows, preferred_element_type=jnp.float32)
-            * score_scale
-        )
-        key_grad = (
-            key_grad
-            + jnp.einsum(
-                "hqk,qhd->khd", score_grad, query_block, preferred_element_type=jnp.float32
-            )
-            * score_scale
-        )
-        return ((key_grad, value_grad), query_grad)
-
-    offsets = jnp.arange(group_rows // block, dtype=jnp.int32) * block
-    zeros_rows = jnp.zeros((group_rows, head_count, head_width), jnp.float32)
-    (key_grad, value_grad), query_grad = lax.scan(
-        back_step, (zeros_rows, zeros_rows), (offsets, log_totals)
-    )
-    return (query_grad.reshape(group_rows, head_count, head_width), key_grad, value_grad)
+        mine = ga.at[:, :, att_at(net, net.c, 0, 0)]
+        for m, dst in enumerate((gq, gk, gv, go)):
+            dst[...] = mine[m].astype(f32).T
+
+    def gain_sums():
+        here = net.z
+        for ref, line, then, place in ((sum_z, line_z, sum_x, net.x), (sum_x, line_x, sum_y, net.y), (sum_y, line_y, sum_c, net.c), (sum_c, [net.device(dc=1)], None, None)):
+            sent = [net.send(ref.at[here], ref.at[here], to) for to in line]
+            yield
+            for copy in sent:
+                copy.wait_recv()
+            total = ref[0]
+            for n in range(1, len(line) + 1):
+                total = total + ref[n]
+            if then is None:
+                gains[0:1, :] = total[0:1] / gain[...]
+                gains[1:2, :] = total[1:2]
+            else:
+                then[place] = total
+                here = place
+
+    take_turns({"t": tokens(), "s": gain_sums(), "w": weights()}, "tswtswtswtwsswww")
+    net.finish()
+
+
+def attn_out(da_all, n1_all, w, q, k, v, p, o, table, tok, dh1, gain, mlp_gain_part):
+    bf, f32 = jnp.bfloat16, jnp.float32
+    slab = (4, 256, 128)
+    scratch = [
+        ((GROUP, D), bf), ((GROUP, D), bf), ((4, D, 256), bf), ((2, GROUP, 128), bf), ((2, GROUP, 128), bf), ((2, GROUP, 128), bf),
+        ((2, GROUP, GROUP), bf), ((GROUP, 256), bf), ((2, GROUP, 128), f32), ((2, GROUP, 128), bf), ((GROUP, 768), bf),
+        ((2, GROUP, 128), f32), ((2, GROUP, 128), f32), ((GROUP, D), bf), ((2, ROWS, D), bf), ((4, ROWS, D), bf),
+        ((2, 64, D), bf), ((6, 64, D), bf), ((4, 256, D), bf), ((2, 4) + slab, bf), ((2,) + slab, bf), ((2,) + slab, bf),
+        ((2,) + slab, bf), ((2,) + slab, bf), ((4, 2, D), f32), ((4, 2, D), f32), ((4, 2, D), f32), ((2, 2, D), f32),
+    ]
+    return pl.pallas_call(
+        attn_out_kernel,
+        name="attn_out",
+        out_shape=(
+            jax.ShapeDtypeStruct((ROWS, D), f32),
+            jax.ShapeDtypeStruct((2, D), f32),
+        ) + (jax.ShapeDtypeStruct((ROWS, 256), f32),) * 4,
+        in_specs=[ANY] * 9 + [VMEM] * 4,
+        out_specs=(VMEM,) * 6,
+        scratch_shapes=[pltpu.VMEM(*s) for s in scratch] + [
+            pltpu.SemaphoreType.DMA((64,)),
+            pltpu.SemaphoreType.DMA((64,)),
+            pltpu.SemaphoreType.DMA((9,)),
+        ],
+        compiler_params=pltpu.CompilerParams(collective_id=4, has_side_effects=True, vmem_limit_bytes=58 << 20),
+    )(da_all, n1_all, w, q, k, v, p, o, table, tok, dh1, gain, mlp_gain_part)
 
 
 def shards(
@@ -784,107 +995,16 @@
     down_weight,
     cotangent,
 ):
-    local_rows = tokens.shape[0]
-    group_rows = local_rows * lax.axis_size("tensor")
-    heads_here = query_weight.shape[1] // HEAD_DIM
-    block = min(QBLOCK, group_rows)
-    segment, position = places(lengths[0], group_rows)
-    rot_cos, rot_sin = rotary(position, HEAD_DIM)
-    shape_heads = (group_rows, heads_here, HEAD_DIM)
-    residual = tokens.astype(jnp.float32)
-    normed, factor_attn = scaled_norm(residual, attn_gain)
-    normed_all = lax.all_gather(normed.astype(jnp.bfloat16), "tensor", axis=0, tiled=True)
-    wq_full, wk_full, wv_full, wo_full = (
-        lax.all_gather(query_weight, "dp", axis=0, tiled=True),
-        lax.all_gather(key_weight, "dp", axis=0, tiled=True),
-        lax.all_gather(value_weight, "dp", axis=0, tiled=True),
-        lax.all_gather(out_weight, "dp", axis=0, tiled=True),
+    half_rates = THETA ** (-(np.arange(64, dtype=np.float32) * np.float32(2.0 / HEAD_DIM)))
+    rates = jnp.asarray(np.concatenate([half_rates, half_rates])[None].astype(np.float32))
+    g_all, n1_all, w, q, k, v, p, o, table = attn_in(
+        tokens, cotangent, lengths, attn_gain[None], rates, query_weight, key_weight, value_weight, out_weight
     )
-    query_pre = jnp.dot(normed_all, wq_full, preferred_element_type=jnp.float32).reshape(
-        shape_heads
-    )
-    key_pre = jnp.dot(normed_all, wk_full, preferred_element_type=jnp.float32).reshape(shape_heads)
-    value_rows = (
-        jnp.dot(normed_all, wv_full, preferred_element_type=jnp.float32)
-        .astype(jnp.bfloat16)
-        .reshape(shape_heads)
-    )
-    queries = rotate(query_pre, rot_cos, rot_sin).astype(jnp.bfloat16)
-    key_rows = rotate(key_pre, rot_cos, rot_sin).astype(jnp.bfloat16)
-    attended, log_totals = attention_forward(queries, key_rows, value_rows, segment, block)
-    a_part = contract(attended, wo_full).astype(jnp.bfloat16)
-    groups = [[0, 1, 2, 3], [4, 5, 6, 7]]
-    cotangent_all = lax.all_gather(cotangent, "tensor", axis=0, tiled=True, axis_index_groups=groups)
-    w_all, n2_all, hidden_res = mlp_in(a_part, tokens, mlp_gain[None], gate_weight.T, up_weight.T, down_weight.T)
-    m_part, dn_part, grads = mlp(w_all, n2_all, cotangent_all)
-    output, hidden_grad, branch_all, mlp_gain_part, gate_wg, up_wg, down_wg = mlp_out(
-        m_part, dn_part, grads, hidden_res, mlp_gain[None], cotangent
-    )
-    mlp_gain_part = mlp_gain_part[0]
-    wq_back, wk_back, wv_back, wo_back = (
-        lax.all_gather(query_weight, "dp", axis=0, tiled=True),
-        lax.all_gather(key_weight, "dp", axis=0, tiled=True),
-        lax.all_gather(value_weight, "dp", axis=0, tiled=True),
-        lax.all_gather(out_weight, "dp", axis=0, tiled=True),
-    )
-    attended_grad = (
-        jnp.dot(branch_all, wo_back, preferred_element_type=jnp.float32)
-        .astype(jnp.bfloat16)
-        .reshape(shape_heads)
-    )
-    query_grad_rot, key_grad_rot, value_grad = attention_backward(
-        queries, key_rows, value_rows, segment, log_totals, attended_grad, block
-    )
-    query_grad = (
-        rotate_back(query_grad_rot, rot_cos, rot_sin).astype(jnp.bfloat16).reshape(group_rows, -1)
-    )
-    key_grad = (
-        rotate_back(key_grad_rot, rot_cos, rot_sin).astype(jnp.bfloat16).reshape(group_rows, -1)
-    )
-    value_grad = value_grad.astype(jnp.bfloat16).reshape(group_rows, -1)
-    out_wgrad = outer_sum(branch_all, attended)
-    query_wgrad = outer_sum(normed_all, query_grad)
-    key_wgrad = outer_sum(normed_all, key_grad)
-    value_wgrad = outer_sum(normed_all, value_grad)
-    normed_part = (
-        contract(query_grad, wq_back) + contract(key_grad, wk_back) + contract(value_grad, wv_back)
-    )
-    normed_grad = lax.psum_scatter(
-        normed_part.astype(jnp.bfloat16), "tensor", scatter_dimension=0, tiled=True
-    ).astype(jnp.float32)
-    tokens_grad = hidden_grad + norm_back(residual, factor_attn, attn_gain, normed_grad)
-    attn_gain_part = jnp.sum(normed_grad * residual * factor_attn, axis=0)
-    summed = (
-        lax.psum_scatter(
-            query_wgrad.astype(jnp.bfloat16), "dp", scatter_dimension=0, tiled=True
-        ).astype(jnp.float32),
-        lax.psum_scatter(
-            key_wgrad.astype(jnp.bfloat16), "dp", scatter_dimension=0, tiled=True
-        ).astype(jnp.float32),
-        lax.psum_scatter(
-            value_wgrad.astype(jnp.bfloat16), "dp", scatter_dimension=0, tiled=True
-        ).astype(jnp.float32),
-        lax.psum_scatter(
-            out_wgrad.astype(jnp.bfloat16), "dp", scatter_dimension=0, tiled=True
-        ).astype(jnp.float32),
-        gate_wg.T,
-        up_wg.T,
-        down_wg.T,
-    )
-    gain_sums = lax.psum((attn_gain_part, mlp_gain_part), ("dp", "tensor"))
-    return (
-        output,
-        tokens_grad,
-        gain_sums[0],
-        summed[0],
-        summed[1],
-        summed[2],
-        summed[3],
-        gain_sums[1],
-        summed[4],
-        summed[5],
-        summed[6],
-    )
+    w_all, n2_all, h1 = mlp_in(o, w[3], tokens, mlp_gain[None], gate_weight.T, up_weight.T, down_weight.T)
+    m_part, dn_part, grads = mlp(w_all, n2_all, g_all)
+    output, dh1, da_all, mlp_gain_part, gate_wg, up_wg, down_wg = mlp_out(m_part, dn_part, grads, h1, mlp_gain[None], cotangent)
+    dx, gains, gq, gk, gv, go = attn_out(da_all, n1_all, w, q, k, v, p, o, table, tokens, dh1, attn_gain[None], mlp_gain_part)
+    return (output, dx, gains[0], gq, gk, gv, go, gains[1], gate_wg.T, up_wg.T, down_wg.T)
 
 
 def solution(mesh):

time: 945 us -> 383 us (0.41)
  waiting for transfers between devices: 494 us -> 0 us
  Pallas kernels: 228 us -> 367 us
  matrix products: 68.8 us -> 0 us
  blocking collectives: 64.5 us -> 0 us
  other arithmetic: 40.3 us -> 0 us
  between operations: 14.8 us -> 0.72 us
    reduce_scatter x5 -> x0, waiting for transfers between devices: 298 us -> none  [the longest x1 69.2 us: shards(): lax.psum_scatter(query_wgrad.astype(jnp.bfloat16), 'dp', scatter_dimensio...]
    all_gather x6 -> x0, waiting for transfers between devices: 193 us -> none  [the longest x1 53.4 us: shards(): lax.all_gather(normed.astype(jnp.bfloat16), 'tensor', axis=0, tiled=True)]
    pallas_call x0 -> x2, Pallas kernels: none -> 143 us  [the longest x1 74.1 us: attn_in(): pl.pallas_call(attn_in_kernel, name='attn_in', out_shape=tuple((jax.Shape...]
    dot_general x26 -> x0, matrix products: 68.8 us -> none  [the longest x4 16.2 us: outer_sum(): lax.dot_general(left, right, (((0,), (0,)), ((), ())), preferred_element_...]
    psum x1 -> x0, blocking collectives: 64.5 us -> none  [shards(): gain_sums = lax.psum((attn_gain_part, mlp_gain_part), ('dp', 'tensor'))]
    convert_element_type x12 -> x0, other arithmetic: 17.1 us -> none  [the longest x4 6.01 us: shards(): summed = (lax.psum_scatter(query_wgrad.astype(jnp.bfloat16), 'dp', scatte...]
  transfers between devices with their start and end apart: 11 -> 0, of which waited for: 10 -> 0; matrix products, arithmetic and copies ran while one was open for 8% -> 0% of each run, Pallas kernels for 9% -> 0%
where the time goes in v2:
time: 383 us
  Pallas kernels  367 us (96%)
  local copies, waits for them, and re-layouts  15.3 us (4%)
    pallas_call x1, Pallas kernels, mlp_out(): pl.pallas_call(mlp_out_kernel, name='mlp_out', out_shape=(jax.ShapeDtypeS...  84.5 us
    pallas_call x1, Pallas kernels, mlp_in(): pl.pallas_call(mlp_in_kernel, name='mlp_in', out_shape=(jax.ShapeDtypeStr...  82.1 us
    pallas_call x1, Pallas kernels, attn_in(): pl.pallas_call(attn_in_kernel, name='attn_in', out_shape=tuple((jax.Shape...  74.1 us
    pallas_call x1, Pallas kernels, attn_out(): pl.pallas_call(attn_out_kernel, name='attn_out', out_shape=(jax.ShapeDtyp...  68.6 us
    pallas_call x1, Pallas kernels, mlp(): pl.pallas_call(mlp_kernel, name='mlp', out_shape=(jax.ShapeDtypeStruct((5...  57.3 us
    unnamed x17, local copies, waits for them, and re-layouts  11.6 us

profile of v2, /device:TPU:1, one launch (start us, length us, event | category | flops | bytes accessed | tf_op | source)
XLA Modules:
  0.0 382.7 jit_solution(14222490344568988207)
XLA Ops:
  0.6 74.1 %attn_in.1 = (bf16[512,2048]{1,0:T(8,128)(2,1)}, bf16[1024,2048]{1,0:T(8,128)(2,1)}, bf16[4,2048,256]{2,1,0:T(8,128)(2,1)}, bf16[2,1024,128]{2,1,0:T(8,128)(2,1)...) custom-call(bf16[128,2048]{1,0:T(8,128)(2,1)} %tok.5, ...), custom_call_target="tpu_custom_call" | custom-call | tf_op jit(solution)/shard_map/attn_in/pallas_call | solution.py:792
  74.8 2.3 slice_bitcast_fusion.wo
  77.0 82.1 %mlp_in.1 = (bf16[3,2,688,2048]{3,2,1,0:T(8,128)(2,1)}, bf16[512,2048]{1,0:T(8,128)(2,1)}, f32[128,2048]{1,0:T(8,128)}) custom-call(bf16[1024,256]{1,0:T(8,128)(2,1)} %get-tuple-element.39.o.o_in, bf16[2048,256]{1,0:T(8,128)(2,1)} %slice_bitcast_fusion.wo, bf16[128,2048]{1,0:T(8,128)(2,1)} %tok.5, f32[1,2048]{1,0:T(1,128)} %bitcast.18, ...), custom_call_target="tpu_custom_call" | custom-call | tf_op jit(solution)/shard_map/mlp_in/pallas_call | solution.py:430
  159.2 57.3 %mlp.1 = (bf16[512,2048]{1,0:T(8,128)(2,1)}, bf16[512,2048]{1,0:T(8,128)(2,1)}, bf16[3,2,688,2048]{3,2,1,0:T(8,128)(2,1)}) custom-call(bf16[3,2,688,2048]{3,2,1,0:T(8,128)(2,1)} %get-tuple-element.41.w_all, bf16[512,2048]{1,0:T(8,128)(2,1)} %get-tuple-element.42.n2_all, bf16[512,2048]{1,0:T(8,128)(2,1)} %get-tuple-element.43.g_all), custom_call_target="tpu_custom_call" | custom-call | flops 25999998976 | bytes 41943040 | tf_op jit(solution)/shard_map/mlp/pallas_call | solution.py:523
  216.5 84.5 %mlp_out.1 = (bf16[128,2048]{1,0:T(8,128)(2,1)}, f32[128,2048]{1,0:T(8,128)}, bf16[1024,2048]{1,0:T(8,128)(2,1)}, f32[1,2048]{1,0:T(1,128)}, f32[688,128]{1,0:T(...) custom-call(bf16[512,2048]{1,0:T(8,128)(2,1)} %get-tuple-element.44.m_part, bf16[512,2048]{1,0:T(8,128)(2,1)} %get-tuple-element.45.dn_part, ...), custom_call_target="tpu_custom_call" | custom-call | tf_op jit(solution)/shard_map/mlp_out/pallas_call | solution.py:622
  301.0 0.0 copy-start
  301.0 68.6 %attn_out.1 = (f32[128,2048]{1,0:T(8,128)}, f32[2,2048]{1,0:T(2,128)}, f32[128,256]{1,0:T(8,128)}, f32[128,256]{1,0:T(8,128)}, f32[128,256]{1,0:T(8,128)}, /*index=5*/f32[128,256]{1,0:T(8,128)}) custom-call(bf16[1024,2048]{1,0:T(8,128)(2,1)} %get-tuple-element.49.da_in, bf16[1024,2048]{1,0:T(8,128)(2,1)} %get-tuple-element.50.n1_in, ...), custom_call_target="tpu_custom_call" | custom-call | tf_op jit(solution)/shard_map/attn_out/pallas_call | solution.py:966
  369.6 0.0 copy-start.3
  369.6 0.0 copy-start.2
  369.6 0.0 copy-start.1
  369.7 1.4 fusion
  371.1 0.0 copy-done
  371.1 0.8 copy.33
  371.9 2.3 copy.34
  374.2 1.6 copy.35
  375.8 1.6 copy.36
  377.3 1.6 copy.37
  378.9 1.6 copy.38
  380.5 0.0 copy-done.3
  380.5 0.7 copy.39
  381.2 0.0 copy-done.2
  381.2 0.7 copy.40
  381.9 0.0 copy-done.1
  381.9 0.7 copy.41
Async XLA Ops:
  301.0 70.1 %copy-start = (bf16[128,2048]{1,0:T(8,128)(2,1)S(1)}, bf16[128,2048]{1,0:T(8,128)(2,1)}, u32[]{:S(2)}) copy-start(bf16[128,2048]{1,0:T(8,128)(2,1)} %get-tuple-element.80) | copy-start | bytes 1572868
  369.6 10.8 %copy-start.3 = (f32[688,128]{1,0:T(8,128)S(1)}, f32[688,128]{1,0:T(8,128)}, u32[]{:S(2)}) copy-start(f32[688,128]{1,0:T(8,128)} %get-tuple-element.64) | copy-start | bytes 1056772
  369.6 11.6 %copy-start.2 = (f32[688,128]{1,0:T(8,128)S(1)}, f32[688,128]{1,0:T(8,128)}, u32[]{:S(2)}) copy-start(f32[688,128]{1,0:T(8,128)} %get-tuple-element.65) | copy-start | bytes 1056772
  369.6 12.3 %copy-start.1 = (f32[688,128]{1,0:T(8,128)S(1)}, f32[688,128]{1,0:T(8,128)}, u32[]{:S(2)}) copy-start(f32[688,128]{1,0:T(8,128)} %get-tuple-element.66) | copy-start | bytes 1056772

commit v3 on v2

v3 whole, which is shorter than its diff:
```python
import functools

import jax
import jax.numpy as jnp
import numpy as np
from jax import lax
from jax.experimental import pallas as pl
from jax.experimental.pallas import tpu as pltpu
from jax.sharding import PartitionSpec as P

HEAD_DIM = 128
EPS = 1e-05
THETA = 10000.0
D = 2048
ROWS = 128
GROUP = 1024
FFB = 688
QROWS = 256
MESH = pl.DeviceIdType.MESH
ANY = pl.BlockSpec(memory_space=pl.ANY)
VMEM = pl.BlockSpec(memory_space=pltpu.VMEM)
NT = (((1,), (1,)), ((), ()))
TN = (((0,), (0,)), ((), ()))


class Net:
    def __init__(self, send_sems, recv_sems):
        dp, t = lax.axis_index("dp"), lax.axis_index("tensor")
        self.y, self.c = lax.div(dp, 4), lax.rem(dp, 2)
        self.xl, self.z = lax.div(t, 4), lax.rem(t, 4)
        self.x = lax.rem(lax.div(dp, 2), 2) * 2 + self.xl
        self.dp, self.t = dp, t
        self.send_sems, self.recv_sems = send_sems, recv_sems
        self.used = 0
        self.sent = []

    def device(self, dx=0, dy=0, dz=0, dc=0):
        x, y = lax.rem(self.x + dx + 4, 4), lax.rem(self.y + dy + 4, 4)
        z, c = lax.rem(self.z + dz + 4, 4), lax.rem(self.c + dc, 2)
        return (y * 4 + lax.div(x, 2) * 2 + c, lax.rem(x, 2) * 4 + z)

    @property
    def beside(self):
        return (self.dp, (1 - self.xl) * 4 + self.z)

    @property
    def across(self):
        return self.device(dx=2)

    def along(self, first):
        on_x = self.c == (0 if first else 1)
        both = []
        for step in (1, -1):
            by_x, by_y = self.device(dx=step), self.device(dy=step)
            both.append(tuple(jnp.where(on_x, u, v) for u, v in zip(by_x, by_y)))
        return both

    def send(self, src, dst, to):
        k = self.used
        self.used += 1
        copy = pltpu.make_async_remote_copy(
            src_ref=src,
            dst_ref=dst,
            send_sem=self.send_sems.at[k],
            recv_sem=self.recv_sems.at[k],
            device_id=to,
            device_id_type=MESH,
        )
        copy.start()
        self.sent.append(copy)
        return copy

    def flush(self):
        for copy in self.sent:
            copy.wait_send()
        self.sent = []

    def greet(self, devices):
        barrier = pltpu.get_barrier_semaphore()
        for device in devices:
            pl.semaphore_signal(barrier, inc=1, device_id=device, device_id_type=MESH)
        pl.semaphore_wait(barrier, len(devices))


def block(z):
    return pl.ds(pl.multiple_of(lax.rem(z + 8, 4) * ROWS, ROWS), ROWS)


def half(z, k):
    return pl.ds(pl.multiple_of(lax.rem(z + 8, 4) * ROWS + k * 64, 64), 64)


def block8(xl, z):
    return pl.ds(pl.multiple_of((xl * 4 + lax.rem(z + 8, 4)) * ROWS, ROWS), ROWS)


def half8(xl, z, k):
    return pl.ds(pl.multiple_of((xl * 4 + lax.rem(z + 8, 4)) * ROWS + k * 64, 64), 64)


def add_rows(rows, dst, *terms):
    def step(i, _):
        at = pl.ds(pl.multiple_of(i * 16, 16), 16)
        total = terms[0][at, :].astype(jnp.float32)
        for term in terms[1:]:
            total = total + term[at, :].astype(jnp.float32)
        dst[at, :] = total.astype(dst.dtype)
        return 0

    lax.fori_loop(0, rows // 16, step, 0)


def gather_z(net, own, dst, arrived=None):
    up, down = net.device(dz=1), net.device(dz=-1)
    z = net.z
    here = arrived or (lambda z: None)
    a0 = net.send(own, dst.at[block(z), :], up)
    a1 = net.send(own, dst.at[block(z), :], down)
    here(z)
    yield
    a0.wait_recv()
    b0 = net.send(dst.at[half(z - 1, 0), :], dst.at[half(z - 1, 0), :], up)
    a1.wait_recv()
    b1 = net.send(dst.at[half(z + 1, 1), :], dst.at[half(z + 1, 1), :], down)
    here(z - 1)
    here(z + 1)
    yield
    b0.wait_recv()
    b1.wait_recv()
    here(z + 2)


def reduce_z(net, part, sums, got, cols=pl.ds(0, D)):
    up, down = net.device(dz=1), net.device(dz=-1)
    z = net.z
    c0 = net.send(part.at[half(z + 2, 0), cols], got.at[0, :, cols], up)
    c1 = net.send(part.at[half(z + 2, 1), cols], got.at[1, :, cols], down)
    d1 = net.send(part.at[half(z + 1, 1), cols], got.at[3, :, cols], up)
    d2 = net.send(part.at[half(z - 1, 0), cols], got.at[4, :, cols], down)
    yield
    c0.wait_recv()
    add_rows(64, sums.at[0, :, cols], part.at[half(z + 1, 0), cols], got.at[0, :, cols])
    d0 = net.send(sums.at[0, :, cols], got.at[2, :, cols], up)
    c1.wait_recv()
    add_rows(64, sums.at[1, :, cols], part.at[half(z - 1, 1), cols], got.at[1, :, cols])
    d3 = net.send(sums.at[1, :, cols], got.at[5, :, cols], down)
    yield
    for copy in (d0, d1, d2, d3):
        copy.wait_recv()


def reduced(net, part, got, at, k):
    here = pl.ds(pl.multiple_of(at - 64 * k, 16), 16)
    total = part[pl.ds(pl.multiple_of(net.z * ROWS + at, 16), 16), :].astype(jnp.float32)
    return total + got[2 + k, here, :].astype(jnp.float32) + got[4 + k, here, :].astype(jnp.float32)


def gather_8(net, own, dst):
    up, down, beside = net.device(dz=1), net.device(dz=-1), net.beside
    xl, z = net.xl, net.z
    place = dst.at[block8(xl, z), :]
    s0 = net.send(own, place, up)
    s1 = net.send(own, place, down)
    s2 = net.send(own, place, beside)
    yield
    s0.wait_recv()
    ref = dst.at[half8(xl, z - 1, 0), :]
    s5 = net.send(ref, ref, up)
    s1.wait_recv()
    ref = dst.at[half8(xl, z + 1, 1), :]
    s6 = net.send(ref, ref, down)
    s2.wait_recv()
    ref = dst.at[block8(1 - xl, z), :]
    s3 = net.send(ref, ref, up)
    s4 = net.send(ref, ref, down)
    yield
    s5.wait_recv()
    s6.wait_recv()
    ref = dst.at[block8(xl, z + 2), :]
    s7 = net.send(ref, ref, beside)
    yield
    s3.wait_recv()
    s4.wait_recv()
    s7.wait_recv()


def reduce_8(net, make, part, sums, got, sums_half, got_half, out):
    up, down, beside = net.device(dz=1), net.device(dz=-1), net.beside
    xl, z = net.xl, net.z
    make(1 - xl, z + 2)
    a = net.send(part.at[block8(1 - xl, z + 2), :], got.at[0], beside)
    make(1 - xl, z + 1)
    b0 = net.send(part.at[block8(1 - xl, z + 1), :], got.at[1], up)
    make(1 - xl, z - 1)
    b1 = net.send(part.at[block8(1 - xl, z - 1), :], got.at[2], down)
    make(xl, z + 2)
    make(xl, z + 1)
    d1 = net.send(part.at[half8(xl, z + 1, 1), :], got_half.at[3], up)
    make(xl, z - 1)
    d2 = net.send(part.at[half8(xl, z - 1, 0), :], got_half.at[4], down)
    make(1 - xl, z)
    make(xl, z)
    yield
    a.wait_recv()
    add_rows(128, sums.at[0], part.at[block8(xl, z + 2), :], got.at[0])
    c0 = net.send(sums.at[0, pl.ds(0, 64), :], got_half.at[0], up)
    c1 = net.send(sums.at[0, pl.ds(64, 64), :], got_half.at[1], down)
    yield
    b0.wait_recv()
    b1.wait_recv()
    add_rows(128, sums.at[1], part.at[block8(1 - xl, z), :], got.at[1], got.at[2])
    e = net.send(sums.at[1], got.at[3], beside)
    yield
    c0.wait_recv()
    add_rows(64, sums_half.at[0], part.at[half8(xl, z + 1, 0), :], got_half.at[0])
    d0 = net.send(sums_half.at[0], got_half.at[2], up)
    c1.wait_recv()
    add_rows(64, sums_half.at[1], part.at[half8(xl, z - 1, 1), :], got_half.at[1])
    d3 = net.send(sums_half.at[1], got_half.at[5], down)
    yield
    for copy in (e, d0, d1, d2, d3):
        copy.wait_recv()

    def rows(at, k):
        here = pl.ds(pl.multiple_of(at - 64 * k, 16), 16)
        total = part[pl.ds(pl.multiple_of(net.t * ROWS + at, 16), 16), :].astype(jnp.float32)
        total = total + got[3, pl.ds(pl.multiple_of(at, 16), 16), :].astype(jnp.float32)
        return total + got_half[2 + k, here, :].astype(jnp.float32) + got_half[4 + k, here, :].astype(jnp.float32)

    out.append(rows)


def each_half(step):
    for k in (0, 1):
        def body(i, _, k=k):
            step(pl.multiple_of(k * 64 + i * 16, 16), k)
            return 0

        lax.fori_loop(0, 4, body, 0)


def gather_plane(net, slab, cut, first, second):
    low, high = cut
    sib = net.device(dc=1)
    second_up, second_down = second

    def share(i, j):
        ref = slab(i, j)
        return net.send(ref, ref, sib)

    def go(i):
        ref = slab(i, 0)
        return net.send(ref, ref, second_up), net.send(ref, ref, second_down)

    shared, halves = [], {}
    own = slab(0, 0)
    ring = len(first) == 2
    round_ = [net.send(own, own, to) for to in first]
    sent = {0: go(0)}
    shared.append(share(0, 0))

    def on(i):
        sent[i][0].wait_recv()
        ref = low(slab(i, -1))
        h0 = net.send(ref, ref, second_up)
        sent[i][1].wait_recv()
        ref = high(slab(i, 1))
        halves[i] = (h0, net.send(ref, ref, second_down))
        shared.append(share(i, -1))
        shared.append(share(i, 1))

    yield
    if ring:
        round_[0].wait_recv()
        ref = low(slab(-1, 0))
        f0 = net.send(ref, ref, first[0])
        round_[1].wait_recv()
        ref = high(slab(1, 0))
        f1 = net.send(ref, ref, first[1])
        for i in (-1, 1):
            sent[i] = go(i)
            shared.append(share(i, 0))
        yield
        on(0)
        yield
        f0.wait_recv()
        f1.wait_recv()
        sent[2] = go(2)
        shared.append(share(2, 0))
    else:
        round_[0].wait_recv()
        sent[1] = go(1)
        shared.append(share(1, 0))
        yield
        on(0)
    for i in list(sent)[1:]:
        yield
        on(i)
    for i in sent:
        yield
        halves[i][0].wait_recv()
        halves[i][1].wait_recv()
        shared.append(share(i, 2))
    yield
    for copy in shared:
        copy.wait_recv()


def reduce_plane(net, mine, other, from_sib, got_half, got_up, got_down, last_bufs, cut, add, first, second):
    low, high = cut
    sib = net.device(dc=1)
    up, down = second
    ring = len(first) == 2
    steps = (0, 1, 3, 2) if ring else (0, 1)
    shared = {}
    for j in (2, 1, 3, 0):
        for i in steps:
            shared[i, j] = net.send(other(i, j), from_sib(i, j), sib)
    yield
    halves, full = {}, {}
    for i in steps:
        shared[i, 2].wait_recv()
        add(None, mine(i, 2), from_sib(i, 2))
        halves[i] = (
            net.send(low(mine(i, 2)), low(got_half(i)), up),
            net.send(high(mine(i, 2)), high(got_half(i)), down),
        )
        yield
    for i in steps:
        for j in (1, 3):
            shared[i, j].wait_recv()
            add(None, mine(i, j), from_sib(i, j))
        halves[i][0].wait_recv()
        add(0, mine(i, 1), got_half(i))
        u = net.send(mine(i, 1), got_up(i), up)
        halves[i][1].wait_recv()
        add(1, mine(i, 3), got_half(i))
        full[i] = (u, net.send(mine(i, 3), got_down(i), down))
        yield
    last = {}
    for i in reversed(steps):
        shared[i, 0].wait_recv()
        full[i][0].wait_recv()
        full[i][1].wait_recv()
        add(None, mine(i, 0), from_sib(i, 0), got_up(i), got_down(i))
        if ring and i == 2:
            ref, to = mine(2, 0), last_bufs(2)
            last[2] = (net.send(low(ref), low(to), first[0]), net.send(high(ref), high(to), first[1]))
        if ring and i == 3:
            last[2][1].wait_recv()
            add(1, mine(3, 0), last_bufs(2))
            last[3] = net.send(mine(3, 0), last_bufs(1), first[1])
        if ring and i == 1:
            last[2][0].wait_recv()
            add(0, mine(1, 0), last_bufs(2))
        if i == 1:
            last[1] = net.send(mine(1, 0), last_bufs(0), first[0])
        yield
    last[1].wait_recv()
    if ring:
        last[3].wait_recv()
        add(None, mine(0, 0), last_bufs(0), last_bufs(1))
    else:
        add(None, mine(0, 0), last_bufs(0))


ATT_CUT = (lambda ref: ref.at[:, pl.ds(0, 64), :], lambda ref: ref.at[:, pl.ds(64, 64), :])


def add_in(cut, total):
    def add(part, dst, *terms):
        begin, n = {None: (0, total), 0: (0, cut), 1: (cut, total - cut)}[part]

        def piece(at, size):
            here = pl.ds(at, size)
            value = dst[here, :].astype(jnp.float32)
            for term in terms:
                value = value + term[here, :].astype(jnp.float32)
            dst[here, :] = value.astype(dst.dtype)

        def step(i, _):
            piece(pl.multiple_of(begin + i * 160, 16), 160)
            return 0

        lax.fori_loop(0, n // 160, step, 0)
        if n % 160:
            piece(begin + n // 160 * 160, n % 160)

    return add


def cut_at(cut, total):
    return (lambda ref: ref.at[pl.ds(0, cut), :], lambda ref: ref.at[pl.ds(cut, total - cut), :])


OD, OD_CUT = 944, 480
GU, GU_CUT = 1376, 688
QKV, QKV_CUT = 768, 384


def plane_slab(net, ref, kind, i, j):
    x = lax.rem(net.x + jnp.where(kind == 0, i, j) + 4, 4)
    y = lax.rem(net.y + jnp.where(kind == 0, j, i) + 4, 4)
    at = pl.ds(pl.multiple_of((y * 4 + lax.div(x, 2) * 2 + kind) * 128, 128), 128)
    return ref.at[lax.rem(x, 2), :, at]


def att_at(net, kind, i, j):
    x, y = lax.rem(net.x + 2 * i + 4, 4), lax.rem(net.y + j + 4, 4)
    return pl.ds(pl.multiple_of((y * 4 + lax.div(x, 2) * 2 + kind) * 128, 128), 128)


def forward(chain, times=1):
    for _ in range(times):
        next(chain, None)


def end(*chains):
    for chain in chains:
        for _ in chain:
            pass


def start(copies):
    for copy in copies:
        copy.start()
    return copies


def sequence_starts(lengths, at, rows):
    index = lax.broadcasted_iota(jnp.int32, (rows, 1), 0) + at
    limit, first = lengths[0, 0], jnp.zeros((rows, 1), jnp.int32)
    for s in range(8):
        first = jnp.where(index >= limit, limit, first)
        if s < 7:
            limit = limit + lengths[0, s + 1]
    return index, first


def params(collective, mib=58):
    return pltpu.CompilerParams(collective_id=collective, has_side_effects=True, vmem_limit_bytes=mib << 20)


def sems(n, local):
    return [pltpu.SemaphoreType.DMA((n,)), pltpu.SemaphoreType.DMA((n,)), pltpu.SemaphoreType.DMA((local,))]


def attn_in_kernel(tok, cot, lengths, gain, rates, wq, wk, wv, wo, wd,
                   g_all, n1_out, w_out, q_out, k_out, v_out, p_out, table_out, o_out, od_out,
                   n1, wo_turned, n1_all, w, q, k, v, p, table, o, send_sems, recv_sems, local):
    net = Net(send_sems, recv_sems)
    own_rows = att_at(net, net.c, 0, 0)
    own_od = plane_slab(net, od_out, net.c, 0, 0)
    wo_turned[...] = wo[...].T
    copies = start(
        [pltpu.make_async_copy(u, w.at[m, own_rows, :], local.at[m]) for m, u in enumerate((wq, wk, wv))]
        + [
            pltpu.make_async_copy(wo_turned, own_od.at[pl.ds(0, 256), :], local.at[3]),
            pltpu.make_async_copy(wd, own_od.at[pl.ds(256, FFB), :], local.at[4]),
        ]
    )
    saves = start([pltpu.make_async_copy(cot, g_all.at[block(net.z), :], local.at[5])])

    def norm(at, _):
        here = pl.ds(at, 16)
        value = tok[here, :].astype(jnp.float32)
        r = lax.rsqrt(jnp.mean(value * value, axis=-1, keepdims=True) + EPS)
        n1[here, :] = (value * r * gain[...]).astype(jnp.bfloat16)

    each_half(norm)
    net.greet([net.device(dx=s) for s in (1, 2, 3)] + [net.device(dy=1), net.device(dy=-1), net.device(dz=1), net.device(dz=-1), net.device(dc=1)])
    place = pltpu.make_async_copy(n1, n1_all.at[block8(net.xl, net.z), :], local.at[6])
    place.start()
    tokens = gather_8(net, n1, n1_all)
    cotangent = gather_z(net, cot, g_all)
    weights = gather_plane(net, lambda i, j: w.at[:, att_at(net, net.c, i, j), :], ATT_CUT, (net.across,), (net.device(dy=1), net.device(dy=-1)))
    later = gather_plane(net, lambda i, j: plane_slab(net, od_out, net.c, i, j), cut_at(OD_CUT, OD), net.along(True), net.along(False))
    forward(tokens)
    for copy in copies:
        copy.wait()
    forward(weights)
    forward(later)

    def tables(i, _):
        at = pl.multiple_of(i * 128, 128)
        index, first = sequence_starts(lengths, at, 128)
        angle = (index - first).astype(jnp.float32) * rates[...]
        lane = lax.broadcasted_iota(jnp.int32, (128, 128), 1)
        table[0, pl.ds(at, 128), :] = jnp.cos(angle)
        sin = jnp.sin(angle)
        table[1, pl.ds(at, 128), :] = jnp.where(lane < 64, -sin, sin)
        return 0

    lax.fori_loop(0, 8, tables, 0)
    forward(tokens)
    forward(weights)
    forward(tokens)
    forward(weights, 2)
    forward(later)
    end(tokens)
    place.wait()
    forward(cotangent)
    end(weights)
    saves += start(
        [
            pltpu.make_async_copy(n1_all, n1_out, local.at[7]),
            pltpu.make_async_copy(w, w_out, local.at[8]),
            pltpu.make_async_copy(table, table_out, local.at[9]),
        ]
    )

    def project(i, _):
        here = pl.ds(pl.multiple_of(i * QROWS, QROWS), QROWS)
        left = n1_all[here, :]
        cos, sin = table[0, here, :], table[1, here, :]
        for m, dst in ((0, q), (1, k)):
            u = jnp.dot(left, w[m], preferred_element_type=jnp.float32)
            for h in range(2):
                uh = u[:, h * 128 : h * 128 + 128]
                dst[h, here, :] = (uh * cos + pltpu.roll(uh, 64, 1) * sin).astype(jnp.bfloat16)
        u = jnp.dot(left, w[2], preferred_element_type=jnp.float32).astype(jnp.bfloat16)
        for h in range(2):
            v[h, here, :] = u[:, h * 128 : h * 128 + 128]
        return 0

    lax.fori_loop(0, GROUP // QROWS, project, 0)
    saves += start([pltpu.make_async_copy(src, dst, local.at[10 + n]) for n, (src, dst) in enumerate(((q, q_out), (k, k_out), (v, v_out)))])
    forward(later)
    forward(cotangent)

    def attend(b):
        rows = slice(b * QROWS, b * QROWS + QROWS)
        first, last = max(0, b - 2) * QROWS, (b + 1) * QROWS
        index, begin = sequence_starts(lengths, b * QROWS, QROWS)
        key = lax.broadcasted_iota(jnp.int32, (QROWS, last - first), 1) + first
        allowed = (key <= index) & (key >= begin)
        for h in range(2):
            s = lax.dot_general(q[h, rows, :], k[h, first:last, :], NT, preferred_element_type=jnp.float32)
            s = jnp.where(allowed, s * HEAD_DIM ** (-0.5), -1e30)
            e = jnp.exp(s - jnp.max(s, axis=-1, keepdims=True))
            weights_b = (e / jnp.sum(e, axis=-1, keepdims=True)).astype(jnp.bfloat16)
            p[h, rows, first:last] = weights_b
            o[rows, h * 128 : h * 128 + 128] = jnp.dot(
                weights_b, v[h, first:last, :], preferred_element_type=jnp.float32
            ).astype(jnp.bfloat16)
        at = (slice(None), pl.ds(b * QROWS, QROWS), pl.ds(first, last - first))
        saves.extend(start([pltpu.make_async_copy(p.at[at], p_out.at[at], local.at[13 + b])]))

    def exchange(n):
        src = o.at[pl.ds(pl.multiple_of((1 - net.xl) * 512 + n * QROWS, QROWS), QROWS), :]
        return net.send(src, o_out.at[net.xl, pl.ds(n * QROWS, QROWS), :], net.beside)

    attend(0)
    forward(later)
    attend(2)
    turn = [exchange(0)]
    forward(later)
    attend(1)
    forward(later)
    attend(3)
    turn.append(exchange(1))
    kept = o.at[pl.ds(pl.multiple_of(net.xl * 512, 512), 512), :]
    saves += start([pltpu.make_async_copy(kept, o_out.at[net.xl], local.at[17])])
    end(later, cotangent)
    for copy in turn:
        copy.wait_recv()
    for copy in saves:
        copy.wait()
    net.flush()


def attn_in(tok, cot, lengths, gain, rates, wq, wk, wv, wo, wd):
    bf, f32 = jnp.bfloat16, jnp.float32
    shapes = (
        ((4 * ROWS, D), bf), ((GROUP, D), bf), ((3, D, 256), bf), ((2, GROUP, 128), bf), ((2, GROUP, 128), bf),
        ((2, GROUP, 128), bf), ((2, GROUP, GROUP), bf), ((2, GROUP, 128), f32), ((2, 512, 256), bf), ((2, OD, D), bf),
    )
    return pl.pallas_call(
        attn_in_kernel,
        name="attn_in",
        out_shape=tuple(jax.ShapeDtypeStruct(*s) for s in shapes),
        in_specs=[VMEM, VMEM, pl.BlockSpec(memory_space=pltpu.SMEM), VMEM, VMEM, ANY, ANY, ANY, VMEM, ANY],
        out_specs=(ANY,) * 10,
        scratch_shapes=[pltpu.VMEM((ROWS, D), bf), pltpu.VMEM((256, 128), bf)] + [pltpu.VMEM(*s) for s in shapes[1:8]] + [pltpu.VMEM((GROUP, 256), bf)] + sems(80, 18),
        compiler_params=params(3),
    )(tok, cot, lengths, gain, rates, wq, wk, wv, wo, wd)


def mlp_kernel(o_in, od_in, wg, wu, tok, cot, g_in, gain,
               h1, dh1, do_out, m_out, od_grad, gain_part, gu_grad,
               w1, w2, o, n2, g, part, m_part, hid, dgate, dup, turned, da, do, sums_a, got_a, sums_d, got_d,
               sib, got_half, got_up, got_down, last, send_sems, recv_sems, local):
    net = Net(send_sems, recv_sems)
    bf, f32 = jnp.bfloat16, jnp.float32
    own = plane_slab(net, w2, net.c, 0, 0)
    early = start(
        [pltpu.make_async_copy(o_in, o, local.at[0]), pltpu.make_async_copy(od_in.at[:, pl.ds(0, 256), :], w1.at[:, pl.ds(0, 256), :], local.at[1])]
    )
    copies = start([pltpu.make_async_copy(u, own.at[pl.ds(n * FFB, FFB), :], local.at[2 + n]) for n, u in enumerate((wg, wu))])
    late = start(
        [pltpu.make_async_copy(g_in, g, local.at[4]), pltpu.make_async_copy(od_in.at[:, pl.ds(256, FFB), :], w1.at[:, pl.ds(256, FFB), :], local.at[5])]
    )
    net.greet([net.device(dx=1), net.device(dx=-1), net.device(dy=1), net.device(dy=-1), net.device(dz=1), net.device(dz=-1), net.device(dc=1)])
    for copy in early:
        copy.wait()

    def branch(z):
        here = block(z)
        u = jnp.dot(o[0, here, :], w1[0, :256, :], preferred_element_type=f32)
        u = u + jnp.dot(o[1, here, :], w1[1, :256, :], preferred_element_type=f32)
        part[here, :] = u.astype(bf)

    for step in (2, 1, -1, 0):
        branch(net.z + step)
    summed = reduce_z(net, part, sums_a, got_a)
    forward(summed)
    for copy in copies:
        copy.wait()
    weights = gather_plane(net, lambda i, j: plane_slab(net, w2, net.c, i, j), cut_at(GU_CUT, GU), net.along(True), net.along(False))
    forward(weights)
    for copy in late:
        copy.wait()

    def hidden_grad(b):
        for at, n in TILES:
            u = lax.dot_general(g[...], w1[b, 256 + at : 256 + at + n, :], NT, preferred_element_type=f32)
            dgate[b, :, at : at + n] = u.astype(bf)

    hidden_grad(0)
    forward(summed)
    forward(weights)
    hidden_grad(1)
    forward(weights)
    end(summed)

    def norm(at, k):
        here = pl.ds(at, 16)
        h = tok[here, :].astype(f32) + reduced(net, part, got_a, at, k)
        h1[here, :] = h
        r = lax.rsqrt(jnp.mean(h * h, axis=-1, keepdims=True) + EPS)
        n2[pl.ds(pl.multiple_of(net.z * ROWS + at, 16), 16), :] = (h * r * gain[...]).astype(bf)

    each_half(norm)
    normed = gather_z(net, n2.at[block(net.z), :], n2)
    forward(normed)
    forward(weights, 2)
    forward(normed)
    forward(weights, 3)
    end(normed)
    end(weights)
    net.flush()

    def ahead(b, _):
        for at, n in TILES:
            gate = lax.dot_general(n2[...], w2[b, at : at + n, :], NT, preferred_element_type=f32)
            up = lax.dot_general(n2[...], w2[b, FFB + at : FFB + at + n, :], NT, preferred_element_type=f32)
            dh = dgate[b, :, at : at + n].astype(f32)
            sig = jax.nn.sigmoid(gate)
            act = gate * sig
            for k, (dst, value) in enumerate(
                ((dgate, dh * up * sig * (1.0 + gate * (1.0 - sig))), (dup, dh * act), (hid, act * up))
            ):
                value = value.astype(bf)
                dst[b, :, at : at + n] = value
                turned[k, b, at : at + n, :] = value.T
        return 0

    lax.fori_loop(0, 2, ahead, 0)

    def back(i, _):
        at = pl.ds(pl.multiple_of(i * 256, 256), 256)
        d = jnp.dot(dgate[0], w2[0, :FFB, at], preferred_element_type=f32)
        d = d + jnp.dot(dgate[1], w2[1, :FFB, at], preferred_element_type=f32)
        d = d + jnp.dot(dup[0], w2[0, FFB:, at], preferred_element_type=f32)
        d = d + jnp.dot(dup[1], w2[1, FFB:, at], preferred_element_type=f32)
        part[:, at] = d.astype(bf)
        return 0

    lax.fori_loop(0, 4, back, 0)
    back_a = reduce_z(net, part, sums_d, got_d, pl.ds(0, D // 2))
    forward(back_a)
    lax.fori_loop(4, 8, back, 0)
    back_b = reduce_z(net, part, sums_d, got_d, pl.ds(D // 2, D // 2))
    forward(back_b)

    def outer(i, _):
        at = pl.ds(pl.multiple_of(i * 512, 512), 512)
        right = n2[:, at]
        for m in range(2):
            for b in range(2):
                w2[b, m * FFB : m * FFB + FFB, at] = jnp.dot(turned[m, b], right, preferred_element_type=f32).astype(bf)
        return 0

    lax.fori_loop(0, 4, outer, 0)
    grads = reduce_plane(
        net, lambda i, j: plane_slab(net, w2, net.c, i, j), lambda i, j: plane_slab(net, w2, 1 - net.c, i, j), lambda i, j: sib.at[i, j],
        lambda i: got_half.at[i], lambda i: got_up.at[i], lambda i: got_down.at[i], lambda i: last.at[i],
        cut_at(GU_CUT, GU), add_in(GU_CUT, GU), net.along(True), net.along(False),
    )
    forward(grads)
    forward(back_a)

    def mixed_part(i, _):
        at = pl.ds(pl.multiple_of(i * 256, 256), 256)
        u = jnp.dot(hid[0], w1[0, 256:, at], preferred_element_type=f32)
        u = u + jnp.dot(hid[1], w1[1, 256:, at], preferred_element_type=f32)
        m_part[:, at] = u.astype(bf)
        return 0

    lax.fori_loop(0, 8, mixed_part, 0)
    saves = start([pltpu.make_async_copy(m_part, m_out, local.at[6])])
    forward(back_b)
    forward(grads, 2)

    def outer_down(i, _):
        at = pl.ds(pl.multiple_of(i * 512, 512), 512)
        for b in range(2):
            w1[b, 256:, at] = jnp.dot(turned[2, b], g[:, at], preferred_element_type=f32).astype(bf)
        return 0

    lax.fori_loop(0, 4, outer_down, 0)
    saves += start([pltpu.make_async_copy(w1.at[:, pl.ds(256, FFB), :], od_grad.at[:, pl.ds(256, FFB), :], local.at[7])])
    forward(grads, 2)
    end(back_a, back_b)
    gain_part[...] = jnp.zeros_like(gain_part)

    def norm_back(at, k):
        here = pl.ds(at, 16)
        h = h1[here, :]
        r = lax.rsqrt(jnp.mean(h * h, axis=-1, keepdims=True) + EPS)
        d = reduced(net, part, got_d, at, k)
        inner = d * gain[...]
        grad = r * inner - h * (r * r * r) * jnp.mean(h * inner, axis=-1, keepdims=True)
        grad = cot[here, :].astype(f32) + grad
        dh1[here, :] = grad
        da[pl.ds(pl.multiple_of(net.z * ROWS + at, 16), 16), :] = grad.astype(bf)
        gain_part[...] += jnp.sum(d * h * r, axis=0, keepdims=True)

    each_half(norm_back)
    turn = []

    def back_out(z):
        here = block(z)
        for b in range(2):
            do[b, here, :] = lax.dot_general(da[here, :], w1[b, :256, :], NT, preferred_element_type=f32).astype(bf)
        rows = pl.ds(pl.multiple_of(net.xl * 512 + lax.rem(z + 8, 4) * ROWS, ROWS), ROWS)
        turn.append(net.send(do.at[1 - net.xl, here, :], do_out.at[rows, :], net.beside))
        saves.extend(start([pltpu.make_async_copy(do.at[net.xl, here, :], do_out.at[rows, :], local.at[8 + len(turn)])]))

    branch_grad = gather_z(net, da.at[block(net.z), :], da, back_out)
    forward(branch_grad)
    forward(grads, 2)
    forward(branch_grad)
    forward(grads, 2)
    end(branch_grad)

    def outer_out(i, _):
        at = pl.ds(pl.multiple_of(i * 512, 512), 512)
        for b in range(2):
            w1[b, :256, at] = lax.dot_general(o[b], da[:, at], TN, preferred_element_type=f32).astype(bf)
        return 0

    lax.fori_loop(0, 4, outer_out, 0)
    saves += start([pltpu.make_async_copy(w1.at[:, pl.ds(0, 256), :], od_grad.at[:, pl.ds(0, 256), :], local.at[8])])
    end(grads)
    gu_grad[...] = plane_slab(net, w2, net.c, 0, 0)[...]
    for copy in turn:
        copy.wait_recv()
    for copy in saves:
        copy.wait()
    net.flush()


TILES = ((0, 256), (256, 256), (512, 176))


def mlp(o, od, wg, wu, tok, cot, g_all, gain):
    bf, f32 = jnp.bfloat16, jnp.float32
    slab = (GU, 128)
    scratch = [
        ((2, OD, D), bf), ((2, GU, D), bf), ((2, 512, 256), bf), ((512, D), bf), ((512, D), bf), ((512, D), bf), ((512, D), bf),
        ((2, 512, FFB), bf), ((2, 512, FFB), bf), ((2, 512, FFB), bf), ((3, 2, FFB, 512), bf), ((512, D), bf), ((2, 512, 256), bf),
        ((2, 64, D), bf), ((6, 64, D), bf), ((2, 64, D), bf), ((6, 64, D), bf),
        ((4, 4) + slab, bf), ((4,) + slab, bf), ((4,) + slab, bf), ((4,) + slab, bf), ((3,) + slab, bf),
    ]
    outs = (((ROWS, D), f32), ((ROWS, D), f32), ((GROUP, 256), bf), ((512, D), bf), ((2, OD, D), bf), ((1, D), f32), (slab, bf))
    return pl.pallas_call(
        mlp_kernel,
        name="mlp",
        out_shape=tuple(jax.ShapeDtypeStruct(*s) for s in outs),
        in_specs=[ANY, ANY, ANY, ANY, VMEM, VMEM, ANY, VMEM],
        out_specs=(VMEM, VMEM, ANY, ANY, ANY, VMEM, VMEM),
        scratch_shapes=[pltpu.VMEM(*s) for s in scratch] + sems(112, 13),
        compiler_params=params(1, 62),
    )(o, od, wg, wu, tok, cot, g_all, gain)


def attn_out_kernel(do_in, n1_in, w_in, q_in, k_in, v_in, p_in, table_in, m_in, od_in, tok, h1, dh1, gain, mlp_gain_part,
                    mixed, dx, gains, qkv_grad, od_grad,
                    do, n1, w, q, k, v, p, table, dqkv, dk, dv, part, sums, got, sums_half, got_half,
                    ga, sib, slab_half, slab_up, slab_down, slab_last, sum_z, sum_x, sum_y, sum_c,
                    m_part, sums_m, got_m, od, od_sib, od_half, od_up, od_down, od_last,
                    send_sems, recv_sems, local):
    net = Net(send_sems, recv_sems)
    bf, f32 = jnp.bfloat16, jnp.float32
    loads = start(
        [
            pltpu.make_async_copy(src, dst, local.at[m])
            for m, (src, dst) in enumerate(((do_in, do), (v_in, v), (p_in, p), (q_in, q), (k_in, k), (table_in, table), (m_in, m_part), (w_in, w), (n1_in, n1)))
        ]
    )
    slabs = start(
        [
            pltpu.make_async_copy(plane_slab(net, od_in, net.c, i, j), od.at[i, j], local.at[9 + n])
            for n, (i, j) in enumerate((i, j) for j in (2, 1, 3, 0) for i in (0, 1, 3, 2))
        ]
    )
    line_x = [net.device(dx=s) for s in (1, 2, 3)]
    line_y = [net.device(dy=s) for s in (1, 2, 3)]
    line_z = [net.device(dz=s) for s in (1, 2, 3)]
    net.greet(line_x + line_y + line_z + [net.device(dc=1)])
    early = reduce_plane(
        net, lambda i, j: od.at[i, j], lambda i, j: plane_slab(net, od_in, 1 - net.c, i, j), lambda i, j: od_sib.at[i, j],
        lambda i: od_half.at[i], lambda i: od_up.at[i], lambda i: od_down.at[i], lambda i: od_last.at[i],
        cut_at(OD_CUT, OD), add_in(OD_CUT, OD), net.along(True), net.along(False),
    )
    forward(early)
    for copy in loads[:7]:
        copy.wait()
    mixing = reduce_z(net, m_part, sums_m, got_m)
    forward(mixing)
    for copy in slabs:
        copy.wait()
    forward(early, 2)

    def attend_back(h, b):
        rows = slice(b * QROWS, b * QROWS + QROWS)
        first, last = max(0, b - 2) * QROWS, (b + 1) * QROWS
        keys, old = slice(first, last), slice(first, b * QROWS)
        weights_b = p[h, rows, keys]
        do_b = do[rows, h * 128 : h * 128 + 128]
        dp = lax.dot_general(do_b, v[h, keys, :], NT, preferred_element_type=f32)
        wide = weights_b.astype(f32)
        centre = jnp.sum(wide * dp, axis=-1, keepdims=True)
        ds = (wide * (dp - centre)).astype(bf)
        dvb = lax.dot_general(weights_b, do_b, TN, preferred_element_type=f32)
        dkb = lax.dot_general(ds, q[h, rows, :], TN, preferred_element_type=f32)
        if b > 0:
            dv[h, old, :] += dvb[: b * QROWS - first]
            dk[h, old, :] += dkb[: b * QROWS - first]
        dv[h, rows, :] = dvb[b * QROWS - first :]
        dk[h, rows, :] = dkb[b * QROWS - first :]
        dqb = jnp.dot(ds, k[h, keys, :], preferred_element_type=f32) * HEAD_DIM ** (-0.5)
        dqb = dqb * table[0, rows, :] - pltpu.roll(dqb, 64, 1) * table[1, rows, :]
        dqkv[rows, h * 128 : h * 128 + 128] = dqb.astype(bf)

    for b in range(GROUP // QROWS):
        for h in range(2):
            attend_back(h, b)
        forward(early)
        if b == 1:
            forward(mixing)

    def turn(i, _):
        here = pl.ds(pl.multiple_of(i * QROWS, QROWS), QROWS)
        for h in range(2):
            u = dk[h, here, :] * HEAD_DIM ** (-0.5)
            u = u * table[0, here, :] - pltpu.roll(u, 64, 1) * table[1, here, :]
            dqkv[here, 256 + h * 128 : 384 + h * 128] = u.astype(bf)
            dqkv[here, 512 + h * 128 : 640 + h * 128] = dv[h, here, :].astype(bf)
        return 0

    lax.fori_loop(0, GROUP // QROWS, turn, 0)
    for copy in loads[7:]:
        copy.wait()
    sum_z[net.z, 0:1, :] = jnp.zeros((1, D), f32)
    sum_z[net.z, 1:2, :] = mlp_gain_part[...]

    def make(xl, z):
        here = block8(xl, z)
        left = dqkv[here, :]

        def columns(i, _):
            at = pl.ds(pl.multiple_of(i * 512, 512), 512)
            u = lax.dot_general(left[:, :256], w[0, at, :], NT, preferred_element_type=f32)
            u = u + lax.dot_general(left[:, 256:512], w[1, at, :], NT, preferred_element_type=f32)
            u = u + lax.dot_general(left[:, 512:], w[2, at, :], NT, preferred_element_type=f32)
            part[here, at] = u.astype(bf)
            sum_z[net.z, 0:1, at] += jnp.sum(u * n1[here, at].astype(f32), axis=0, keepdims=True)
            return 0

        lax.fori_loop(0, 4, columns, 0)

    out = []
    tokens = reduce_8(net, make, part, sums, got, sums_half, got_half, out)
    forward(tokens)

    def outer(i, _):
        at = pl.ds(pl.multiple_of(i * 256, 256), 256)
        ga[:, at] = lax.dot_general(dqkv[...], n1[:, at], TN, preferred_element_type=f32).astype(bf)
        return 0

    lax.fori_loop(0, 8, outer, 0)

    def slab(kind):
        return lambda i, j: ga.at[:, att_at(net, kind, i, j)]

    weights = reduce_plane(
        net, slab(net.c), slab(1 - net.c), lambda i, j: sib.at[i, j], lambda i: slab_half.at[i], lambda i: slab_up.at[i],
        lambda i: slab_down.at[i], lambda i: slab_last.at[i], cut_at(QKV_CUT, QKV), add_in(QKV_CUT, QKV), (net.across,), (net.device(dy=1), net.device(dy=-1)),
    )

    def gain_sums():
        here = net.z
        for ref, line, then, place in ((sum_z, line_z, sum_x, net.x), (sum_x, line_x, sum_y, net.y), (sum_y, line_y, sum_c, net.c), (sum_c, [net.device(dc=1)], None, None)):
            sent = [net.send(ref.at[here], ref.at[here], to) for to in line]
            yield
            for copy in sent:
                copy.wait_recv()
            total = ref[0]
            for n in range(1, len(line) + 1):
                total = total + ref[n]
            if then is None:
                gains[0:1, :] = total[0:1] / gain[...]
                gains[1:2, :] = total[1:2]
            else:
                then[place] = total
                here = place

    sums_of_gains = gain_sums()
    forward(tokens)
    forward(weights)
    forward(sums_of_gains)
    forward(early)
    forward(tokens)
    forward(weights)
    forward(early)
    forward(sums_of_gains)
    forward(tokens)
    forward(weights)
    end(mixing)

    def mix(at, k):
        here = pl.ds(at, 16)
        mixed[here, :] = (h1[here, :] + reduced(net, m_part, got_m, at, k)).astype(bf)

    each_half(mix)
    forward(sums_of_gains)
    forward(weights)
    end(early)
    od_grad[...] = od[0, 0]
    forward(sums_of_gains)
    end(tokens)

    def step(at, k):
        here = pl.ds(at, 16)
        value = tok[here, :].astype(f32)
        r = lax.rsqrt(jnp.mean(value * value, axis=-1, keepdims=True) + EPS)
        inner = out[0](at, k) * gain[...]
        dx[here, :] = dh1[here, :] + r * inner - value * (r * r * r) * jnp.mean(value * inner, axis=-1, keepdims=True)

    each_half(step)
    end(weights, sums_of_gains)
    qkv_grad[...] = slab(net.c)(0, 0)[...]
    net.flush()


def attn_out(do, n1, w, q, k, v, p, table, m, od, tok, h1, dh1, gain, mlp_gain_part):
    bf, f32 = jnp.bfloat16, jnp.float32
    slab, slab_od = (QKV, 128), (OD, 128)
    scratch = [
        ((GROUP, 256), bf), ((GROUP, D), bf), ((3, D, 256), bf), ((2, GROUP, 128), bf), ((2, GROUP, 128), bf), ((2, GROUP, 128), bf),
        ((2, GROUP, GROUP), bf), ((2, GROUP, 128), f32), ((GROUP, QKV), bf),
        ((2, GROUP, 128), f32), ((2, GROUP, 128), f32), ((GROUP, D), bf), ((2, ROWS, D), bf), ((4, ROWS, D), bf),
        ((2, 64, D), bf), ((6, 64, D), bf), ((QKV, D), bf), ((2, 4) + slab, bf), ((2,) + slab, bf), ((2,) + slab, bf),
        ((2,) + slab, bf), ((1,) + slab, bf), ((4, 2, D), f32), ((4, 2, D), f32), ((4, 2, D), f32), ((2, 2, D), f32),
        ((512, D), bf), ((2, 64, D), bf), ((6, 64, D), bf), ((4, 4) + slab_od, bf), ((4, 4) + slab_od, bf),
        ((4,) + slab_od, bf), ((4,) + slab_od, bf), ((4,) + slab_od, bf), ((3,) + slab_od, bf),
    ]
    outs = (((ROWS, D), bf), ((ROWS, D), f32), ((2, D), f32), (slab, bf), (slab_od, bf))
    return pl.pallas_call(
        attn_out_kernel,
        name="attn_out",
        out_shape=tuple(jax.ShapeDtypeStruct(*s) for s in outs),
        in_specs=[ANY] * 10 + [VMEM] * 5,
        out_specs=(VMEM,) * 5,
        scratch_shapes=[pltpu.VMEM(*s) for s in scratch] + sems(112, 25),
        compiler_params=params(4),
    )(do, n1, w, q, k, v, p, table, m, od, tok, h1, dh1, gain, mlp_gain_part)


def finish_kernel(mixed_in, dx_in, gains, qkv, od, gu, mixed, dx, ag, gq, gk, gv, go, mg, gg, gu_out, gd):
    f32 = jnp.float32
    mixed[...] = mixed_in[...]
    dx[...] = dx_in[...]
    ag[...] = gains[0:1, :]
    mg[...] = gains[1:2, :]
    for n, dst in enumerate((gq, gk, gv)):
        dst[...] = qkv[n * 256 : n * 256 + 256, :].astype(f32).T
    go[...] = od[:256, :].astype(f32).T
    gd[...] = od[256:, :].astype(f32)
    gg[...] = gu[:FFB, :].astype(f32)
    gu_out[...] = gu[FFB:, :].astype(f32)


def finish(mixed, dx, gains, qkv, od, gu):
    f32 = jnp.float32
    outs = (
        ((ROWS, D), jnp.bfloat16), ((ROWS, D), f32), ((1, D), f32), ((ROWS, 256), f32), ((ROWS, 256), f32), ((ROWS, 256), f32),
        ((ROWS, 256), f32), ((1, D), f32), ((FFB, 128), f32), ((FFB, 128), f32), ((FFB, 128), f32),
    )
    return pl.pallas_call(
        finish_kernel,
        name="finish",
        out_shape=tuple(jax.ShapeDtypeStruct(*s) for s in outs),
        in_specs=[VMEM] * 6,
        out_specs=(VMEM,) * 11,
        compiler_params=pltpu.CompilerParams(vmem_limit_bytes=32 << 20),
    )(mixed, dx, gains, qkv, od, gu)


def shards(
    tokens,
    lengths,
    attn_gain,
    query_weight,
    key_weight,
    value_weight,
    out_weight,
    mlp_gain,
    gate_weight,
    up_weight,
    down_weight,
    cotangent,
):
    half_rates = THETA ** (-(np.arange(64, dtype=np.float32) * np.float32(2.0 / HEAD_DIM)))
    rates = jnp.asarray(np.concatenate([half_rates, half_rates])[None].astype(np.float32))
    g_all, n1_all, w, q, k, v, p, table, o, od = attn_in(
        tokens, cotangent, lengths, attn_gain[None], rates, query_weight, key_weight, value_weight, out_weight, down_weight.T
    )
    h1, dh1, do, m, od_part, gain_part, gu = mlp(o, od, gate_weight.T, up_weight.T, tokens, cotangent, g_all, mlp_gain[None])
    mixed, dx, gains, qkv, od_grad = attn_out(do, n1_all, w, q, k, v, p, table, m, od_part, tokens, h1, dh1, attn_gain[None], gain_part)
    mixed, dx, ag, gq, gk, gv, go, mg, gg, gu, gd = finish(mixed, dx, gains, qkv, od_grad, gu)
    return (mixed, dx, ag[0], gq, gk, gv, go, mg[0], gg.T, gu.T, gd.T)


def solution(mesh):
    return jax.shard_map(
        shards,
        mesh=mesh,
        in_specs=(
            P(("dp", "tensor"), None),
            P("dp", None),
            P(),
            P("dp", "tensor"),
            P("dp", "tensor"),
            P("dp", "tensor"),
            P("dp", "tensor"),
            P(),
            P("dp", "tensor"),
            P("dp", "tensor"),
            P("dp", "tensor"),
            P(("dp", "tensor"), None),
        ),
        out_specs=(
            P(("dp", "tensor"), None),
            P(("dp", "tensor"), None),
            P(),
            P("dp", "tensor"),
            P("dp", "tensor"),
            P("dp", "tensor"),
            P("dp", "tensor"),
            P(),
            P("dp", "tensor"),
            P("dp", "tensor"),
            P("dp", "tensor"),
        ),
        check_vma=False,
    )
```

time: 383 us -> 287 us (0.75)
  Pallas kernels: 367 us -> 281 us
  local copies, waits for them, and re-layouts: 15.3 us -> 4.85 us
    pallas_call x4 -> x3, Pallas kernels: 293 us -> 211 us  [the longest x1 127 us: mlp(): pl.pallas_call(mlp_kernel, name='mlp', out_shape=tuple((jax.ShapeDtypeStr...]
    unnamed x17 -> x12, local copies, waits for them, and re-layouts: 11.6 us -> 4.85 us
    pallas_call x1, Pallas kernels: 74.1 us -> 69.2 us  [attn_in(): pl.pallas_call(attn_in_kernel, name='attn_in', out_shape=tuple((jax.Shape...]
where the time goes in v3:
time: 287 us; the launch traced here: 286 us
  Pallas kernels  281 us (98%)
  local copies, waits for them, and re-layouts  4.85 us (2%)
    pallas_call x1, Pallas kernels, mlp(): pl.pallas_call(mlp_kernel, name='mlp', out_shape=tuple((jax.ShapeDtypeStr...  127 us
    pallas_call x1, Pallas kernels, attn_out(): pl.pallas_call(attn_out_kernel, name='attn_out', out_shape=tuple((jax.Sha...  82.5 us
    pallas_call x1, Pallas kernels, attn_in(): pl.pallas_call(attn_in_kernel, name='attn_in', out_shape=tuple((jax.Shape...  69.2 us

profile of v3, /device:TPU:1, one launch (start us, length us, event | category | flops | bytes accessed | tf_op | source)
XLA Modules:
  0.0 286.2 jit_solution(13310908984998897349)
XLA Ops:
  0.6 69.2 %attn_in.1 = (bf16[512,2048]{1,0:T(8,128)(2,1)}, bf16[1024,2048]{1,0:T(8,128)(2,1)}, bf16[3,2048,256]{2,1,0:T(8,128)(2,1)}, bf16[2,1024,128]{2,1,0:T(8,128)(2,1)...) custom-call(bf16[128,2048]{1,0:T(8,128)(2,1)} %tok.5, ...), custom_call_target="tpu_custom_call" | custom-call | tf_op jit(solution)/shard_map/attn_in/pallas_call | solution.py:578
  69.8 127.2 %mlp.1 = (f32[128,2048]{1,0:T(8,128)}, f32[128,2048]{1,0:T(8,128)}, bf16[1024,256]{1,0:T(8,128)(2,1)}, bf16[512,2048]{1,0:T(8,128)(2,1)}, bf16[2,944,2048]{2,1,0...) custom-call(bf16[2,512,256]{2,1,0:T(8,128)(2,1)} %get-tuple-element.44.o_in, ...), custom_call_target="tpu_custom_call" | custom-call | tf_op jit(solution)/shard_map/mlp/pallas_call | solution.py:787
  197.0 0.0 copy-start.2
  197.0 82.5 %attn_out.1 = (bf16[128,2048]{1,0:T(8,128)(2,1)}, f32[128,2048]{1,0:T(8,128)}, f32[2,2048]{1,0:T(2,128)}, bf16[768,128]{1,0:T(8,128)(2,1)}, bf16[944,128]{1,0:T(8,128)(2,1)}) custom-call(bf16[1024,256]{1,0:T(8,128)(2,1)} %get-tuple-element.47.do_in, bf16[1024,2048]{1,0:T(8,128)(2,1)} %get-tuple-element.48.n1_in, ...), custom_call_target="tpu_custom_call" | custom-call | tf_op jit(solution)/shard_map/attn_out/pallas_call | solution.py:981
  279.5 0.0 copy-done.2
  279.5 0.0 copy-start
  279.5 1.2 copy-done
  280.8 0.0 copy-start.1
  280.8 1.0 copy-done.1
  281.8 0.0 copy-start.3
  281.8 0.9 copy-done.3
  282.7 0.0 copy-start.4
  282.7 0.9 copy-done.4
  283.7 0.0 copy-start.5
  283.7 0.7 copy-done.5
  284.4 1.8 finish.1
Async XLA Ops:
  197.0 82.5 %copy-start.2 = (bf16[1376,128]{1,0:T(8,128)(2,1)S(1)}, bf16[1376,128]{1,0:T(8,128)(2,1)}, u32[]{:S(2)}) copy-start(bf16[1376,128]{1,0:T(8,128)(2,1)} %get-tuple-element.65.gu) | copy-start | bytes 1056772
  279.5 1.2 copy-start
  280.8 1.0 copy-start.1
  281.8 0.9 copy-start.3
  282.7 0.9 copy-start.4
  283.7 0.7 copy-start.5
